TPU v7x, 32 devices: a whole 2x2x4 slice. The times are simulated.
32 devices in a mesh: fsdp: 16 (over z, y, core), seq: 2 (over x).
Axes of the slice: x: 2, y: 2, z: 4, core: 2. Of those that a mesh axis runs over, the one named last changes fastest.
Arguments:
- hidden_in: bfloat16 [8192, 1536], P(('fsdp', 'seq')), may hold values from -6 to 6
- grad_out: bfloat16 [8192, 1536], P(('fsdp', 'seq')), may hold values from -7.5 to 7.5
- routes: int32 [8192, 8], P(('fsdp', 'seq')), may hold values from 0 to 39, all different within a row; in each aligned block of 256 rows (0 to 255, 256 to 511, ...) at most 76 rows name the same one
- gate_weights: bfloat16 [8192, 8], P(('fsdp', 'seq')), may hold values from 0.059814453 to 0.25
- doc_start: int32 [8192], P('fsdp'), may hold values from 0 to 8191, as said below
- qkv_weight: float32 [1536, 2560], P(('fsdp', 'seq')), may hold values from -1.14819832 to 1.14819832
- qkv_first: float32 [1536, 2560], P(('fsdp', 'seq')), may hold values from -24 to 24
- qkv_second: float32 [1536, 2560], P(('fsdp', 'seq')), may hold values from 0.65536 to 10.48576
- out_weight: float32 [1536, 1536], P(None, ('fsdp', 'seq')), may hold values from -3.75 to 3.75
- out_first: float32 [1536, 1536], P(None, ('fsdp', 'seq')), may hold values from -3 to 3
- out_second: float32 [1536, 1536], P(None, ('fsdp', 'seq')), may hold values from 0.01024 to 0.16384
- norm_gains: float32 [2, 1536], P(None, ('fsdp', 'seq')), may hold values from 0.35 to 1.95
- gains_first: float32 [2, 1536], P(None, ('fsdp', 'seq')), may hold values from -96 to 96
- gains_second: float32 [2, 1536], P(None, ('fsdp', 'seq')), may hold values from 9.0112 to 144.1792
- gate_weight: float32 [40, 1536, 512], P('seq', 'fsdp'), may hold values from -0.19136639 to 0.19136639
- gate_first: float32 [40, 1536, 512], P('seq', 'fsdp'), may hold values from -14 to 14
- gate_second: float32 [40, 1536, 512], P('seq', 'fsdp'), may hold values from 0.20475 to 3.276
- up_weight: float32 [40, 1536, 512], P('seq', 'fsdp'), may hold values from -0.19136639 to 0.19136639
- up_first: float32 [40, 1536, 512], P('seq', 'fsdp'), may hold values from -14 to 14
- up_second: float32 [40, 1536, 512], P('seq', 'fsdp'), may hold values from 0.20475 to 3.276
- down_weight: float32 [40, 512, 1536], P('seq', None, 'fsdp'), may hold values from -7.32 to 7.32
- down_first: float32 [40, 512, 1536], P('seq', None, 'fsdp'), may hold values from -0.625 to 0.625
- down_second: float32 [40, 512, 1536], P('seq', None, 'fsdp'), may hold values from 0.0004914 to 0.0078624
Outputs:
- block_output: bfloat16 [8192, 1536], P(('fsdp', 'seq'))
- input_grad: float32 [8192, 1536], P(('fsdp', 'seq'))
- qkv_master: float32 [1536, 2560], P(('fsdp', 'seq'))
- qkv_momentum: float32 [1536, 2560], P(('fsdp', 'seq'))
- qkv_variance: float32 [1536, 2560], P(('fsdp', 'seq'))
- out_master: float32 [1536, 1536], P(None, ('fsdp', 'seq'))
- out_momentum: float32 [1536, 1536], P(None, ('fsdp', 'seq'))
- out_variance: float32 [1536, 1536], P(None, ('fsdp', 'seq'))
- gains_master: float32 [2, 1536], P(None, ('fsdp', 'seq'))
- gains_momentum: float32 [2, 1536], P(None, ('fsdp', 'seq'))
- gains_variance: float32 [2, 1536], P(None, ('fsdp', 'seq'))
- gate_master: float32 [40, 1536, 512], P('seq', 'fsdp')
- gate_momentum: float32 [40, 1536, 512], P('seq', 'fsdp')
- gate_variance: float32 [40, 1536, 512], P('seq', 'fsdp')
- up_master: float32 [40, 1536, 512], P('seq', 'fsdp')
- up_momentum: float32 [40, 1536, 512], P('seq', 'fsdp')
- up_variance: float32 [40, 1536, 512], P('seq', 'fsdp')
- down_master: float32 [40, 512, 1536], P('seq', None, 'fsdp')
- down_momentum: float32 [40, 512, 1536], P('seq', None, 'fsdp')
- down_variance: float32 [40, 512, 1536], P('seq', None, 'fsdp')
- clip_factors: float32 [24], replicated
- lamb_norms: float32 [2, 7], replicated
Inputs may be any that keep to these rules, and one draw needn't show every extreme that they name: doc_start never falls, doc_start[t] <= t, and a document begins at t exactly where doc_start[t] = t; every document has at most 512 tokens and one has exactly 512. `routes`: in the rows of one device no expert is named by more than 76 (token, choice) pairs.
All inputs are finite; a program needn't handle non-finite values.
Results may differ from a plain program's by a relative error of at most 0.023.
The roundings to bfloat16 on the way count: a program that leaves them out, or rounds other values in their place, can miss the bound.
Values may be sent and summed in bfloat16 or wider, within the bound.
A program may use at most 384 MiB of HBM per device.

v0:
```python
import jax
import jax.numpy as jnp
from jax import lax
from jax.sharding import PartitionSpec as P

D = 1536
NH = 24
KVH = 8
HD = 64
EXPERTS = 40
TOP = 8
STEP = 10
CAP = 76


RESIDUAL_SCALE = 0.22
SCORE_SCALE = 0.015625
NORM_EPS = 1e-06
ROPE_BASE = 10000.0
CLIP_BASE = 4.5
BETA_ONE = 0.9
BETA_TWO = 0.999
ADAM_EPS = 1e-06
WEIGHT_DECAY = 0.01
LEARN_RATE = 0.3
MASK_FILL = -1e30


def from_behind(array, axis, by):
    devices = lax.axis_size(axis)
    pairs = [(i, i + by) for i in range(devices) if 0 <= i + by < devices]
    return lax.ppermute(array, axis, pairs)


def joined(value, axis, join):
    pieces = jax.tree.map(lambda part: lax.all_gather(part, axis), value)
    head = jax.tree.map(lambda part: part[0], pieces)
    tail = jax.tree.map(lambda part: part[1:], pieces)
    running, _ = lax.scan(lambda running, slab: (join(running, slab), None), head, tail)
    return running


def rope_tables(positions, head_width):
    half_width = head_width // 2
    frequency = ROPE_BASE ** (-(jnp.arange(half_width, dtype=jnp.float32) * (2.0 / head_width)))
    angles = positions.astype(jnp.float32)[:, None] * frequency[None, :]
    return (jnp.cos(angles), jnp.sin(angles))


def rotate(values, cos_table, sin_table):
    half_width = values.shape[-1] // 2
    view_shape = (cos_table.shape[0],) + (1,) * (values.ndim - 2) + (half_width,)
    cos_view = cos_table.reshape(view_shape)
    sin_view = sin_table.reshape(view_shape)
    first_half = values[..., :half_width]
    second_half = values[..., half_width:]
    return jnp.concatenate(
        [
            first_half * cos_view - second_half * sin_view,
            second_half * cos_view + first_half * sin_view,
        ],
        axis=-1,
    )


def slot_table(routed, expert_count, capacity):
    flat_routes = routed.reshape(-1)
    row_count = flat_routes.shape[0]
    onehot = (flat_routes[:, None] == jnp.arange(expert_count, dtype=jnp.int32)[None, :]).astype(
        jnp.int32
    )
    slot_rank = jnp.sum((jnp.cumsum(onehot, axis=0) - 1) * onehot, axis=1)
    target = flat_routes * capacity + slot_rank
    sources = (
        jnp.full((expert_count * capacity,), row_count, jnp.int32)
        .at[target]
        .set(jnp.arange(row_count, dtype=jnp.int32))
    )
    return (sources, target)


def column_scale(factor):
    per_kv = NH // KVH
    head_part = jnp.repeat(factor.reshape(KVH, per_kv), HD, axis=1)
    return jnp.concatenate([head_part, jnp.ones((KVH, 2 * HD), factor.dtype)], axis=1).reshape(-1)


def adam_direction(weight_now, gradient, mean_old, square_old):
    momentum = BETA_ONE * mean_old + (1.0 - BETA_ONE) * gradient
    variance = BETA_TWO * square_old + (1.0 - BETA_TWO) * gradient * gradient
    direction = (
        momentum / (1.0 - BETA_ONE**STEP) / (jnp.sqrt(variance / (1.0 - BETA_TWO**STEP)) + ADAM_EPS)
        + WEIGHT_DECAY * weight_now
    )
    return (momentum, variance, direction)


def norm_back(values, inverse, gain, grad_normed):
    scaled = grad_normed * gain
    average = jnp.mean(scaled * values, axis=-1, keepdims=True)
    grad_values = inverse * (scaled - values * inverse * inverse * average)
    grad_gain = jnp.sum(grad_normed * values * inverse, axis=0)
    return (grad_values, grad_gain)


def fetch_experts(gate_weight, up_weight, down_weight):
    return (
        lax.all_gather(gate_weight.astype(jnp.bfloat16), "fsdp", axis=1, tiled=True),
        lax.all_gather(up_weight.astype(jnp.bfloat16), "fsdp", axis=1, tiled=True),
        lax.all_gather(down_weight.astype(jnp.bfloat16), "fsdp", axis=2, tiled=True),
    )


def combine_stats(left_part, right_part):
    return (
        left_part[0] + right_part[0],
        left_part[1] + right_part[1],
        jnp.maximum(left_part[2], right_part[2]),
    )


def local(
    hidden_in,
    grad_out,
    routes,
    gate_weights,
    doc_start,
    qkv_weight,
    qkv_first,
    qkv_second,
    out_weight,
    out_first,
    out_second,
    norm_gains,
    gains_first,
    gains_second,
    gate_weight,
    gate_first,
    gate_second,
    up_weight,
    up_first,
    up_second,
    down_weight,
    down_first,
    down_second,
):
    seq_count = lax.axis_size("seq")
    seq_index = lax.axis_index("seq")
    fsdp_index = lax.axis_index("fsdp")
    tok_rows = hidden_in.shape[0]
    group_len = tok_rows * seq_count
    blocks = max(1, group_len // 512)
    qblock = group_len // blocks
    per_kv = NH // KVH
    group_width = (per_kv + 2) * HD
    kv_dev = KVH // seq_count
    heads_dev = kv_dev * per_kv
    exp_dev = EXPERTS // seq_count
    qkv_full, out_full, gains_full = (
        lax.all_gather(qkv_weight.astype(jnp.bfloat16), ("fsdp", "seq"), axis=0, tiled=True),
        lax.all_gather(out_weight.astype(jnp.bfloat16), ("fsdp", "seq"), axis=1, tiled=True),
        lax.all_gather(norm_gains.astype(jnp.bfloat16), ("fsdp", "seq"), axis=1, tiled=True),
    )
    gate_full, up_full, down_full = fetch_experts(gate_weight, up_weight, down_weight)
    attn_gain = gains_full[0].astype(jnp.float32)
    ffn_gain = gains_full[1].astype(jnp.float32)
    hidden = hidden_in.astype(jnp.float32)
    inverse_one = lax.rsqrt(jnp.mean(hidden * hidden, axis=-1, keepdims=True) + NORM_EPS)
    normed_one = (hidden * inverse_one * attn_gain).astype(jnp.bfloat16)
    projected = jnp.dot(normed_one, qkv_full, preferred_element_type=jnp.float32).reshape(
        tok_rows, KVH, group_width
    )
    group_first = fsdp_index * group_len
    token_pos = group_first + seq_index * tok_rows + jnp.arange(tok_rows, dtype=jnp.int32)
    own_starts = lax.dynamic_slice_in_dim(doc_start, seq_index * tok_rows, tok_rows)
    cos_table, sin_table = rope_tables(token_pos - own_starts, HD)
    turned = rotate(
        projected[:, :, : (per_kv + 1) * HD].reshape(tok_rows, KVH, per_kv + 1, HD),
        cos_table,
        sin_table,
    )
    outgoing = jnp.concatenate(
        [turned.reshape(tok_rows, KVH, (per_kv + 1) * HD), projected[:, :, (per_kv + 1) * HD :]],
        axis=2,
    )
    outgoing = outgoing.astype(jnp.bfloat16).reshape(tok_rows, KVH * group_width)
    headwise = lax.all_to_all(outgoing, "seq", split_axis=1, concat_axis=0, tiled=True).reshape(
        group_len, kv_dev, group_width
    )
    queries = headwise[:, :, : per_kv * HD].reshape(group_len, kv_dev, per_kv, HD)
    keyvals = headwise[:, :, per_kv * HD :]
    earlier = from_behind(keyvals, "fsdp", 1)
    both_kv = jnp.concatenate([earlier, keyvals], axis=0)
    keys_all = both_kv[:, :, :HD]
    values_all = both_kv[:, :, HD:]
    key_pos = group_first - group_len + jnp.arange(2 * group_len, dtype=jnp.int32)
    query_pos = group_first + jnp.arange(group_len, dtype=jnp.int32)
    query_blocks = queries.reshape(blocks, qblock, kv_dev, per_kv, HD)
    start_blocks = doc_start.reshape(blocks, qblock)
    pos_blocks = query_pos.reshape(blocks, qblock)

    def forward_block(block_args):
        block_q, block_start, block_pos = block_args
        allowed = (key_pos[None, :] >= block_start[:, None]) & (
            key_pos[None, :] <= block_pos[:, None]
        )
        scores = (
            jnp.einsum("qjid,kjd->jiqk", block_q, keys_all, preferred_element_type=jnp.float32)
            * SCORE_SCALE
        )
        masked = jnp.where(allowed, scores, MASK_FILL)
        row_peak = jnp.max(masked, axis=-1, keepdims=True)
        exponent = jnp.where(allowed, jnp.exp(masked - row_peak), 0.0)
        row_total = jnp.sum(exponent, axis=-1, keepdims=True)
        attn_probs = (exponent / row_total).astype(jnp.bfloat16)
        attn_mixed = jnp.einsum(
            "jiqk,kjd->qjid", attn_probs, values_all, preferred_element_type=jnp.float32
        )
        return (
            attn_mixed.astype(jnp.bfloat16),
            (row_peak + jnp.log(row_total))[..., 0],
            jnp.max(row_peak, axis=(2, 3)),
        )

    attn_mixed, log_totals, block_peaks = lax.map(
        forward_block, (query_blocks, start_blocks, pos_blocks)
    )
    head_peak = jnp.max(block_peaks, axis=0).reshape(heads_dev)
    attn_heads = attn_mixed.reshape(group_len, heads_dev * HD)
    attn_tokens = lax.all_to_all(attn_heads, "seq", split_axis=0, concat_axis=1, tiled=True)
    after_attn = hidden + RESIDUAL_SCALE * jnp.dot(
        attn_tokens, out_full, preferred_element_type=jnp.float32
    )
    inverse_two = lax.rsqrt(jnp.mean(after_attn * after_attn, axis=-1, keepdims=True) + NORM_EPS)
    normed_two = (after_attn * inverse_two * ffn_gain).astype(jnp.bfloat16)
    sources, target = slot_table(routes, EXPERTS, CAP)
    row_count = tok_rows * TOP
    token_of = jnp.where(sources < row_count, sources // TOP, tok_rows)
    zero_row = jnp.zeros((1, D), jnp.bfloat16)
    send_rows = jnp.concatenate([normed_two, zero_row], axis=0)[token_of].reshape(
        seq_count, exp_dev, CAP, D
    )
    send_grads = jnp.concatenate([grad_out, zero_row], axis=0)[token_of].reshape(
        seq_count, exp_dev, CAP, D
    )
    send_gates = jnp.concatenate([gate_weights.reshape(-1), jnp.zeros((1,), jnp.bfloat16)])[
        sources
    ].reshape(seq_count, exp_dev, CAP)
    recv_rows, recv_grads, recv_gates = (
        lax.all_to_all(send_rows, "seq", split_axis=0, concat_axis=0, tiled=True),
        lax.all_to_all(send_grads, "seq", split_axis=0, concat_axis=0, tiled=True),
        lax.all_to_all(send_gates, "seq", split_axis=0, concat_axis=0, tiled=True),
    )
    gate_pre = jnp.einsum(
        "secd,edf->secf", recv_rows, gate_full, preferred_element_type=jnp.float32
    )
    up_pre = jnp.einsum("secd,edf->secf", recv_rows, up_full, preferred_element_type=jnp.float32)
    sigmoid_gate = jax.nn.sigmoid(gate_pre)
    activated = gate_pre * sigmoid_gate
    hidden_act = (activated * up_pre).astype(jnp.bfloat16)
    expert_out = jnp.einsum(
        "secf,efd->secd", hidden_act, down_full, preferred_element_type=jnp.float32
    ).astype(jnp.bfloat16)
    returned = lax.all_to_all(expert_out, "seq", split_axis=0, concat_axis=0, tiled=True)
    picked = (
        returned.reshape(EXPERTS * CAP, D)[target].reshape(tok_rows, TOP, D).astype(jnp.float32)
    )
    mixture = jnp.sum(gate_weights.astype(jnp.float32)[:, :, None] * picked, axis=1)
    block_output = (after_attn + RESIDUAL_SCALE * mixture).astype(jnp.bfloat16)
    gate_full, up_full, down_full = fetch_experts(gate_weight, up_weight, down_weight)
    grad_expert = (
        RESIDUAL_SCALE * recv_gates.astype(jnp.float32)[..., None] * recv_grads.astype(jnp.float32)
    ).astype(jnp.bfloat16)
    down_grad = jnp.einsum(
        "secf,secd->efd", hidden_act, grad_expert, preferred_element_type=jnp.float32
    )
    grad_act = jnp.einsum(
        "secd,efd->secf", grad_expert, down_full, preferred_element_type=jnp.float32
    )
    silu_slope = sigmoid_gate * (1.0 + gate_pre * (1.0 - sigmoid_gate))
    grad_gate_pre = (grad_act * up_pre * silu_slope).astype(jnp.bfloat16)
    grad_up_pre = (grad_act * activated).astype(jnp.bfloat16)
    gate_grad = jnp.einsum(
        "secd,secf->edf", recv_rows, grad_gate_pre, preferred_element_type=jnp.float32
    )
    up_grad = jnp.einsum(
        "secd,secf->edf", recv_rows, grad_up_pre, preferred_element_type=jnp.float32
    )
    grad_rows = (
        jnp.einsum("secf,edf->secd", grad_gate_pre, gate_full, preferred_element_type=jnp.float32)
        + jnp.einsum("secf,edf->secd", grad_up_pre, up_full, preferred_element_type=jnp.float32)
    ).astype(jnp.bfloat16)
    came_back = lax.all_to_all(grad_rows, "seq", split_axis=0, concat_axis=0, tiled=True)
    grad_normed_two = jnp.sum(
        came_back.reshape(EXPERTS * CAP, D)[target].reshape(tok_rows, TOP, D).astype(jnp.float32),
        axis=1,
    )
    back_two, gain_grad_two = norm_back(after_attn, inverse_two, ffn_gain, grad_normed_two)
    grad_after = grad_out.astype(jnp.float32) + back_two
    grad_attn = (RESIDUAL_SCALE * grad_after).astype(jnp.bfloat16)
    out_grad = jnp.einsum("tc,td->cd", attn_tokens, grad_attn, preferred_element_type=jnp.float32)
    grad_mixed = jnp.einsum(
        "td,cd->tc", grad_attn, out_full, preferred_element_type=jnp.float32
    ).astype(jnp.bfloat16)
    grad_heads = lax.all_to_all(grad_mixed, "seq", split_axis=1, concat_axis=0, tiled=True).reshape(
        blocks, qblock, kv_dev, per_kv, HD
    )

    def backward_block(carry_kv, block_args):
        block_q, block_start, block_pos, block_lse, block_grad = block_args
        allowed = (key_pos[None, :] >= block_start[:, None]) & (
            key_pos[None, :] <= block_pos[:, None]
        )
        scores = (
            jnp.einsum("qjid,kjd->jiqk", block_q, keys_all, preferred_element_type=jnp.float32)
            * SCORE_SCALE
        )
        attn_probs = jnp.where(allowed, jnp.exp(scores - block_lse[..., None]), 0.0)
        rounded = attn_probs.astype(jnp.bfloat16)
        grad_probs = jnp.einsum(
            "qjid,kjd->jiqk", block_grad, values_all, preferred_element_type=jnp.float32
        )
        centre = jnp.sum(attn_probs * grad_probs, axis=-1, keepdims=True)
        grad_scores = (attn_probs * (grad_probs - centre)).astype(jnp.bfloat16)
        grad_query = (
            jnp.einsum("jiqk,kjd->qjid", grad_scores, keys_all, preferred_element_type=jnp.float32)
            * SCORE_SCALE
        )
        grad_key = (
            jnp.einsum("jiqk,qjid->kjd", grad_scores, block_q, preferred_element_type=jnp.float32)
            * SCORE_SCALE
        )
        grad_value = jnp.einsum(
            "jiqk,qjid->kjd", rounded, block_grad, preferred_element_type=jnp.float32
        )
        return (carry_kv + jnp.concatenate([grad_key, grad_value], axis=-1), grad_query)

    grad_kv, grad_query = lax.scan(
        backward_block,
        jnp.zeros((2 * group_len, kv_dev, 2 * HD), jnp.float32),
        (query_blocks, start_blocks, pos_blocks, log_totals, grad_heads),
    )
    from_later = from_behind(grad_kv[:group_len].astype(jnp.bfloat16), "fsdp", -1).astype(
        jnp.float32
    )
    own_kv = grad_kv[group_len:] + from_later
    group_cos, group_sin = rope_tables(query_pos - doc_start, HD)
    query_key = jnp.concatenate(
        [grad_query.reshape(group_len, kv_dev, per_kv, HD), own_kv[:, :, None, :HD]], axis=2
    )
    unturned = rotate(query_key, group_cos, -group_sin).reshape(
        group_len, kv_dev, (per_kv + 1) * HD
    )
    grad_headwise = (
        jnp.concatenate([unturned, own_kv[:, :, HD:]], axis=2)
        .astype(jnp.bfloat16)
        .reshape(group_len, kv_dev * group_width)
    )
    grad_projected = lax.all_to_all(grad_headwise, "seq", split_axis=0, concat_axis=1, tiled=True)
    qkv_grad = jnp.einsum(
        "tc,tq->cq", normed_one, grad_projected, preferred_element_type=jnp.float32
    )
    grad_normed_one = jnp.einsum(
        "tq,cq->tc", grad_projected, qkv_full, preferred_element_type=jnp.float32
    )
    back_one, gain_grad_one = norm_back(hidden, inverse_one, attn_gain, grad_normed_one)
    input_grad = grad_after + back_one
    gains_grad = jnp.stack([gain_grad_one, gain_grad_two])
    summed_qkv, summed_out, summed_gains = (
        lax.psum_scatter(qkv_grad, ("fsdp", "seq"), scatter_dimension=0, tiled=True),
        lax.psum_scatter(out_grad, ("fsdp", "seq"), scatter_dimension=1, tiled=True),
        lax.psum_scatter(gains_grad, ("fsdp", "seq"), scatter_dimension=1, tiled=True),
    )
    summed_gate, summed_up, summed_down = (
        lax.psum_scatter(
            gate_grad.astype(jnp.bfloat16), "fsdp", scatter_dimension=1, tiled=True
        ).astype(jnp.float32),
        lax.psum_scatter(
            up_grad.astype(jnp.bfloat16), "fsdp", scatter_dimension=1, tiled=True
        ).astype(jnp.float32),
        lax.psum_scatter(
            down_grad.astype(jnp.bfloat16), "fsdp", scatter_dimension=2, tiled=True
        ).astype(jnp.float32),
    )
    weight_list = [
        qkv_weight,
        out_weight,
        norm_gains[0],
        norm_gains[1],
        gate_weight,
        up_weight,
        down_weight,
    ]
    grad_list = [
        summed_qkv,
        summed_out,
        summed_gains[0],
        summed_gains[1],
        summed_gate,
        summed_up,
        summed_down,
    ]
    mean_list = [
        qkv_first,
        out_first,
        gains_first[0],
        gains_first[1],
        gate_first,
        up_first,
        down_first,
    ]
    square_list = [
        qkv_second,
        out_second,
        gains_second[0],
        gains_second[1],
        gate_second,
        up_second,
        down_second,
    ]
    updates = [
        adam_direction(weight_now, gradient, mean_old, square_old)
        for weight_now, gradient, mean_old, square_old in zip(
            weight_list, grad_list, mean_list, square_list
        )
    ]
    local_weight = jnp.stack([jnp.sum(weight_now * weight_now) for weight_now in weight_list])
    local_step = jnp.stack([jnp.sum(piece[2] * piece[2]) for piece in updates])
    local_peaks = lax.dynamic_update_slice(
        jnp.full((NH,), MASK_FILL, jnp.float32), head_peak, (seq_index * heads_dev,)
    )
    weight_square, step_square, peak_heads = joined(
        (local_weight, local_step, local_peaks), ("fsdp", "seq"), combine_stats
    )
    weight_norm = jnp.sqrt(weight_square)
    step_norm = jnp.sqrt(step_square)
    trust_ratio = weight_norm / step_norm
    masters = [
        weight_list[number] - LEARN_RATE * trust_ratio[number] * updates[number][2]
        for number in range(7)
    ]
    clip_limit = CLIP_BASE * HD**0.5 / 8.0
    clip_factors = clip_limit / jnp.maximum(peak_heads, clip_limit)
    qkv_master = masters[0] * column_scale(clip_factors)[None, :]
    return (
        block_output,
        input_grad,
        qkv_master,
        updates[0][0],
        updates[0][1],
        masters[1],
        updates[1][0],
        updates[1][1],
        jnp.stack([masters[2], masters[3]]),
        jnp.stack([updates[2][0], updates[3][0]]),
        jnp.stack([updates[2][1], updates[3][1]]),
        masters[4],
        updates[4][0],
        updates[4][1],
        masters[5],
        updates[5][0],
        updates[5][1],
        masters[6],
        updates[6][0],
        updates[6][1],
        clip_factors,
        jnp.stack([weight_norm, step_norm]),
    )


def solution(mesh):
    return jax.shard_map(
        local,
        mesh=mesh,
        in_specs=(
            P(("fsdp", "seq"), None),
            P(("fsdp", "seq"), None),
            P(("fsdp", "seq"), None),
            P(("fsdp", "seq"), None),
            P("fsdp"),
            P(("fsdp", "seq"), None),
            P(("fsdp", "seq"), None),
            P(("fsdp", "seq"), None),
            P(None, ("fsdp", "seq")),
            P(None, ("fsdp", "seq")),
            P(None, ("fsdp", "seq")),
            P(None, ("fsdp", "seq")),
            P(None, ("fsdp", "seq")),
            P(None, ("fsdp", "seq")),
            P("seq", "fsdp", None),
            P("seq", "fsdp", None),
            P("seq", "fsdp", None),
            P("seq", "fsdp", None),
            P("seq", "fsdp", None),
            P("seq", "fsdp", None),
            P("seq", None, "fsdp"),
            P("seq", None, "fsdp"),
            P("seq", None, "fsdp"),
        ),
        out_specs=(
            P(("fsdp", "seq"), None),
            P(("fsdp", "seq"), None),
            P(("fsdp", "seq"), None),
            P(("fsdp", "seq"), None),
            P(("fsdp", "seq"), None),
            P(None, ("fsdp", "seq")),
            P(None, ("fsdp", "seq")),
            P(None, ("fsdp", "seq")),
            P(None, ("fsdp", "seq")),
            P(None, ("fsdp", "seq")),
            P(None, ("fsdp", "seq")),
            P("seq", "fsdp", None),
            P("seq", "fsdp", None),
            P("seq", "fsdp", None),
            P("seq", "fsdp", None),
            P("seq", "fsdp", None),
            P("seq", "fsdp", None),
            P("seq", None, "fsdp"),
            P("seq", None, "fsdp"),
            P("seq", None, "fsdp"),
            P(),
            P(),
        ),
        check_vma=False,
    )
```

profile of v0, /device:TPU:0, one launch (start us, length us, event | category | flops | bytes accessed | tf_op | source)
XLA Modules:
  0.0 2522.6 jit_solution(12866874783106181051)
XLA Ops:
  22.4 69.6 %all-gather.2 = bf16[32,48,2]{1,2,0:T(2,128)(2,1)S(1)} all-gather(bf16[1,48,2]{1,2,0:T(2,128)(2,1)S(1)} %convert_bitcast_fusion), channel_id=1, replica_groups=mesh['fsdp'=16,'seq'=2] {'fsdp','seq'}, dimensions={0}, use_global_device_ids=true | all-gather | bytes 6336 | tf_op jit(solution)/shard_map/all_gather | solution.py:162
  92.1 11.3 reduce-window.6
  118.6 17.4 all-to-all-done
  153.7 10.0 fusion.27
  163.7 13.4 fusion.85
  190.1 19.4 gather_fusion.2
  218.9 14.7 gather_fusion
  233.6 11.0 reshape.368
  252.7 14.7 gather_fusion.3
  267.3 11.1 reshape.372
  278.4 78.7 %all-to-all-done.2 = bf16[2,20,76,1536]{3,2,1,0:T(8,128)(2,1)} async-done(((bf16[2,20,76,1536]{3,2,1,0:T(8,128)(2,1)}), bf16[2,20,76,1536]{3,2,1,0:T(8,128)(2,1)}, u32[]{:S(2)}, u32[]{:S(2)}) %all-to-all-start.2) | async-done | bytes 9338912 | tf_op jit(solution)/shard_map/all_to_all | solution.py:250
  357.1 16.4 all-to-all-start.5
  373.7 19.3 fusion.12
  393.0 89.3 %all-gather.16.cloned.1.call-done = bf16[20,1536,512]{2,1,0:T(8,128)(2,1)} async-done(((bf16[20,96,512]{2,1,0:T(8,128)(2,1)}), bf16[20,1536,512]{2,1,0:T(8,128)(2,1)}) %all-gather.16.cloned.1.call-update) | async-done | bytes 31457296 | tf_op jit(solution)/shard_map/all_gather | solution.py:109
  482.3 19.4 fusion.8
  501.7 140.7 %all-gather.18.cloned.1.call-done = bf16[20,512,1536]{1,2,0:T(8,128)(2,1)} async-done(((bf16[20,512,96]{1,2,0:T(8,128)(2,1)}), bf16[20,512,1536]{1,2,0:T(8,128)(2,1)}) %all-gather.18.cloned.1.call-update) | async-done | bytes 31457296 | tf_op jit(solution)/shard_map/all_gather | solution.py:110
  642.5 26.1 %fusion.52 = (bf16[2,20,76,512]{3,2,0,1:T(8,128)(2,1)}, bf16[2,20,76,512]{3,2,0,1:T(8,128)(2,1)S(1)}, bf16[2,20,76,512]{3,2,0,1:T(8,128)(2,1)}) fusion(f32[20,2,76,512]{3,2,1,0:T(8,128)} %fusion.8, f32[20,2,76,512]{3,2,1,0:T(8,128)} %fusion.12, bf16[20,512,1536]{1,2,0:T(8,128)(2,1)} %all-gather.18.cloned.1.call-done, ...), kind=kOutput, calls=%fused_computation.64 | convolution fusion | flops 4818862080 | bytes 62599040 | tf_op jit(solution)/shard_map/secd,efd->secf/dot_general | solution.py:277
  668.5 24.8 fusion.6
  693.4 22.5 fusion.44
  715.9 8.3 copy.140
  731.9 19.3 fusion.41
  759.4 81.0 %all-to-all-done.6 = bf16[2,20,76,1536]{3,2,1,0:T(8,128)(2,1)} async-done(((bf16[2,20,76,1536]{3,2,1,0:T(8,128)(2,1)}), bf16[2,20,76,1536]{3,2,1,0:T(8,128)(2,1)}, u32[]{:S(2)}, u32[]{:S(2)}) %all-to-all-start.6) | async-done | bytes 9338912 | tf_op jit(solution)/shard_map/all_to_all | solution.py:293
  848.0 11.0 reshape.373
  859.0 18.1 gather_fusion.4
  885.5 70.1 %all-to-all-done.3 = bf16[2,20,76,1536]{3,2,1,0:T(8,128)(2,1)} async-done(((bf16[2,20,76,1536]{3,2,1,0:T(8,128)(2,1)}), bf16[2,20,76,1536]{3,2,1,0:T(8,128)(2,1)}, u32[]{:S(2)}, u32[]{:S(2)}) %all-to-all-start.3) | async-done | bytes 9338912 | tf_op jit(solution)/shard_map/all_to_all | solution.py:264
  955.5 11.0 reshape.369
  966.5 18.5 gather_fusion.1
  985.1 9.0 fusion.36
  1004.8 9.4 all-to-all-done.7
  1019.3 12.0 fusion.80
  1031.2 16.9 fusion.18
  1048.2 17.0 fusion.20
  1089.4 13.5 all-to-all-done.8
  1117.6 9.3 fusion.99
  1128.9 19.7 bitcast_convert_fusion.2
  1150.5 19.6 bitcast_convert_fusion.1
  1172.1 20.1 bitcast_convert_fusion
  1193.7 67.4 %all-gather.3 = f32[32,1,24]{2,1,0:T(1,128)S(1)} all-gather(f32[1,1,24]{2,1,0:T(1,128)S(1)} %dynamic_update_slice.17), channel_id=1, replica_groups=mesh['fsdp'=16,'seq'=2] {'fsdp','seq'}, dimensions={0}, use_global_device_ids=true | all-gather | bytes 3168 | tf_op jit(solution)/shard_map/all_gather | solution.py:36
  1265.9 88.8 %reduce-scatter.11.cloned.1.call-done = f32[1536,48]{0,1:T(8,128)} async-done(((f32[1536,1536]{0,1:T(8,128)}), f32[1536,48]{0,1:T(8,128)}) %reduce-scatter.11.cloned.1.call-update) | async-done | bytes 294928 | tf_op jit(solution)/shard_map/reduce_scatter | solution.py:371
  1357.4 173.9 %reduce-scatter.9.cloned.1.call-done = f32[48,2560]{1,0:T(8,128)} async-done(((f32[1536,2560]{1,0:T(8,128)}), f32[48,2560]{1,0:T(8,128)}) %reduce-scatter.9.cloned.1.call-update) | async-done | bytes 491536 | tf_op jit(solution)/shard_map/reduce_scatter | solution.py:370
  1533.6 296.5 %reduce-scatter.13.cloned.1.call-done = bf16[20,96,512]{2,1,0:T(8,128)(2,1)} async-done(((bf16[20,1536,512]{2,1,0:T(8,128)(2,1)}), bf16[20,96,512]{2,1,0:T(8,128)(2,1)}) %reduce-scatter.13.cloned.1.call-update) | async-done | bytes 1966096 | tf_op jit(solution)/shard_map/reduce_scatter | solution.py:375
  1830.1 9.2 multiply_reduce_fusion.2
  1839.3 289.3 %reduce-scatter.15.cloned.1.call-done = bf16[20,96,512]{2,1,0:T(8,128)(2,1)} async-done(((bf16[20,1536,512]{2,1,0:T(8,128)(2,1)}), bf16[20,96,512]{2,1,0:T(8,128)(2,1)}) %reduce-scatter.15.cloned.1.call-update) | async-done | bytes 1966096 | tf_op jit(solution)/shard_map/reduce_scatter | solution.py:378
  2128.6 9.2 multiply_reduce_fusion.1
  2137.7 289.4 %reduce-scatter.17.cloned.1.call-done = bf16[20,512,96]{1,2,0:T(8,128)(2,1)} async-done(((bf16[20,512,1536]{1,2,0:T(8,128)(2,1)}), bf16[20,512,96]{1,2,0:T(8,128)(2,1)}) %reduce-scatter.17.cloned.1.call-update) | async-done | bytes 1966096 | tf_op jit(solution)/shard_map/reduce_scatter | solution.py:381
  2427.2 9.2 multiply_reduce_fusion
  2445.9 39.5 %all-reduce.5 = (f32[224]{0:T(256)S(1)}, f32[224]{0:T(256)S(1)}) all-reduce(f32[224]{0:T(256)S(1)} %dynamic-update-slice, f32[224]{0:T(256)S(1)} %dynamic-update-slice.1), channel_id=2, replica_groups=mesh['fsdp'=16,'seq'=2] {'fsdp','seq'}, use_global_device_ids=true, to_apply=%add.3 | all-reduce | flops 448 | bytes 3584
  2495.5 8.5 multiply_subtract_fusion
  (376 shorter events, 209.4 us)
Async XLA Ops:
  7.2 98.7 %all-gather.10.cloned.1.call-start = ((), (), s32[]{:S(2)}) async-start(), calls=%async_computation.15 | async-start | bytes 8110080 | tf_op jit(solution)/shard_map/all_gather | solution.py:160
  9.0 204.6 %all-gather.12.cloned.1.call-start = ((), (), s32[]{:S(2)}) async-start(), calls=%async_computation.16 | async-start | bytes 4866048 | tf_op jit(solution)/shard_map/all_gather | solution.py:161
  10.7 363.0 %all-gather.14.cloned.1.call-start = ((), (), s32[]{:S(2)}) async-start(), calls=%async_computation.17 | async-start | bytes 33423360 | tf_op jit(solution)/shard_map/all_gather | solution.py:108
  14.5 467.8 %all-gather.16.cloned.1.call-start = ((), (), s32[]{:S(2)}) async-start(), calls=%async_computation.18 | async-start | bytes 33423360 | tf_op jit(solution)/shard_map/all_gather | solution.py:109
  18.2 86.2 %copy-start.54 = (bf16[256,8]{0,1:T(8,128)(2,1)S(1)}, bf16[256,8]{0,1:T(8,128)(2,1)}, u32[]{:S(2)}) copy-start(bf16[256,8]{0,1:T(8,128)(2,1)} %param.28) | copy-start | bytes 12292
  18.2 624.2 %all-gather.18.cloned.1.call-start = ((), (), s32[]{:S(2)}) async-start(), calls=%async_computation.19 | async-start | bytes 33423360 | tf_op jit(solution)/shard_map/all_gather | solution.py:110
  22.0 83.3 %copy-start.59 = (s32[512]{0:T(512)S(1)}, s32[512]{0:T(512)}, u32[]{:S(2)}) copy-start(s32[512]{0:T(512)} %param.29) | copy-start | bytes 6148
  22.0 83.4 %copy-start.23 = (bf16[256,1536]{1,0:T(8,128)(2,1)S(1)}, bf16[256,1536]{1,0:T(8,128)(2,1)}, u32[]{:S(2)}) copy-start(bf16[256,1536]{1,0:T(8,128)(2,1)} %param.25) | copy-start | bytes 2359300
  105.4 112.1 %copy-start.43 = (f32[1536]{0:T(1024)}, f32[1536]{0:T(1024)S(1)}, u32[]{:S(2)}) copy-start(f32[1536]{0:T(1024)S(1)} %get-tuple-element.150) | copy-start | bytes 18436
  114.2 21.7 all-to-all-start
  118.4 45.3 %copy-start.1 = (pred[512,1024]{0,1:T(8,128)(4,1)}, pred[512,1024]{0,1:T(8,128)(4,1)S(1)}, u32[]{:S(2)}) copy-start(pred[512,1024]{0,1:T(8,128)(4,1)S(1)} %compare_and_fusion) | copy-start | bytes 1572868
  144.9 2.9 collective-permute-start
  146.6 35.4 %copy-start.50 = (s32[2048,1]{0,1:T(1,128)}, s32[2048,1]{0,1:T(1,128)S(1)}, u32[]{:S(2)}) copy-start(s32[2048,1]{0,1:T(1,128)S(1)} %compare_select_fusion) | copy-start | bytes 24580
  178.3 35.3 %copy-start.24 = (bf16[256,1536]{1,0:T(8,128)(2,1)S(1)}, bf16[256,1536]{1,0:T(8,128)(2,1)}, u32[]{:S(2)}) copy-start(bf16[256,1536]{1,0:T(8,128)(2,1)} %param.25) | copy-start | bytes 2359300
  178.3 32.0 %all-to-all-start.1 = ((bf16[2,256,768]{1,2,0:T(8,128)(2,1)}), bf16[2,256,768]{1,2,0:T(8,128)(2,1)S(1)}, u32[]{:S(2)}, u32[]{:S(2)}) async-start(bf16[2,256,768]{1,2,0:T(8,128)(2,1)} %copy.128), calls=%async_computation.1 | async-start | bytes 1572864 | tf_op jit(solution)/shard_map/all_to_all | solution.py:230
  210.3 34.4 %all-to-all-start.4 = ((bf16[2,2,760]{2,1,0:T(2,128)(2,1)}), bf16[2,2,760]{2,1,0:T(2,128)(2,1)S(1)}, u32[]{:S(2)}, u32[]{:S(2)}) async-start(bf16[2,2,760]{2,1,0:T(2,128)(2,1)} %reshape.470), calls=%async_computation.4 | async-start | bytes 12288 | tf_op jit(solution)/shard_map/all_to_all | solution.py:252
  244.7 112.4 %all-to-all-start.2 = ((bf16[2,20,76,1536]{3,2,1,0:T(8,128)(2,1)}), bf16[2,20,76,1536]{3,2,1,0:T(8,128)(2,1)}, u32[]{:S(2)}, u32[]{:S(2)}) async-start(bf16[2,20,76,1536]{3,2,1,0:T(8,128)(2,1)} %reshape.368), calls=%async_computation.2 | async-start | bytes 19660800 | tf_op jit(solution)/shard_map/all_to_all | solution.py:250
  357.1 144.6 %all-to-all-start.5 = ((bf16[2,20,76,1536]{3,2,1,0:T(8,128)(2,1)}), bf16[2,20,76,1536]{3,2,1,0:T(8,128)(2,1)}, u32[]{:S(2)}, u32[]{:S(2)}) async-start(bf16[2,20,76,1536]{3,2,1,0:T(8,128)(2,1)} %reshape.372), calls=%async_computation.5 | async-start | bytes 19660800 | tf_op jit(solution)/shard_map/all_to_all | solution.py:251
  373.7 268.8 %copy-start.41 = (f32[2,20,76]{2,1,0:T(8,128)}, f32[2,20,76]{2,1,0:T(8,128)S(1)}, u32[]{:S(2)}) copy-start(f32[2,20,76]{2,1,0:T(8,128)S(1)} %convert_multiply_fusion.8) | copy-start | bytes 36484
  668.5 63.4 %copy-start.5 = (bf16[2,20,76,512]{3,2,0,1:T(8,128)(2,1)}, bf16[2,20,76,512]{3,2,0,1:T(8,128)(2,1)S(1)}, u32[]{:S(2)}) copy-start(bf16[2,20,76,512]{3,2,0,1:T(8,128)(2,1)S(1)} %get-tuple-element.191) | copy-start | bytes 9338884
  724.2 116.2 %all-to-all-start.6 = ((bf16[2,20,76,1536]{3,2,1,0:T(8,128)(2,1)}), bf16[2,20,76,1536]{3,2,1,0:T(8,128)(2,1)}, u32[]{:S(2)}, u32[]{:S(2)}) async-start(bf16[2,20,76,1536]{3,2,1,0:T(8,128)(2,1)} %copy.140), calls=%async_computation.6 | async-start | bytes 19660800 | tf_op jit(solution)/shard_map/all_to_all | solution.py:293
  759.4 88.5 %copy-start.55 = (bf16[256,8]{0,1:T(8,128)(2,1)S(1)}, bf16[256,8]{0,1:T(8,128)(2,1)}, u32[]{:S(2)}) copy-start(bf16[256,8]{0,1:T(8,128)(2,1)} %param.28) | copy-start | bytes 12292
  759.4 88.6 %copy-start.60 = (s32[512]{0:T(512)S(1)}, s32[512]{0:T(512)}, u32[]{:S(2)}) copy-start(s32[512]{0:T(512)} %param.29) | copy-start | bytes 6148
  759.4 88.6 %copy-start.51 = (s32[2048,1]{0,1:T(1,128)S(1)}, s32[2048,1]{0,1:T(1,128)}, u32[]{:S(2)}) copy-start(s32[2048,1]{0,1:T(1,128)} %copy-done.50) | copy-start | bytes 24580
  840.4 115.2 %all-to-all-start.3 = ((bf16[2,20,76,1536]{3,2,1,0:T(8,128)(2,1)}), bf16[2,20,76,1536]{3,2,1,0:T(8,128)(2,1)}, u32[]{:S(2)}, u32[]{:S(2)}) async-start(bf16[2,20,76,1536]{3,2,1,0:T(8,128)(2,1)} %copy.137), calls=%async_computation.3 | async-start | bytes 19660800 | tf_op jit(solution)/shard_map/all_to_all | solution.py:264
  995.6 115.7 %copy-start.13 = (f32[256,1536]{1,0:T(8,128)}, f32[256,1536]{1,0:T(8,128)S(1)}, u32[]{:S(2)}) copy-start(f32[256,1536]{1,0:T(8,128)S(1)} %get-tuple-element.197) | copy-start | bytes 4718596
  1000.0 19.3 copy-start.2
  1000.9 13.3 all-to-all-start.7
  1071.4 4.9 collective-permute-start.1
  1078.2 24.7 copy-start.25
  1078.2 24.7 copy-start.48
  1078.2 24.7 copy-start.58
  1084.8 18.0 all-to-all-start.8
  1089.4 174.8 %reduce-scatter.19.cloned.1.call-start = ((), (), s32[]{:S(2)}) async-start(), calls=%async_computation.25 | async-start | bytes 811008
  1111.2 243.4 %reduce-scatter.11.cloned.1.call-start = ((), (), s32[]{:S(2)}) async-start(), calls=%async_computation.21 | async-start | bytes 9732096 | tf_op jit(solution)/shard_map/reduce_scatter | solution.py:371
  1117.6 413.7 %reduce-scatter.9.cloned.1.call-start = ((), (), s32[]{:S(2)}) async-start(), calls=%async_computation.20 | async-start | bytes 16220160 | tf_op jit(solution)/shard_map/reduce_scatter | solution.py:370
  1126.9 703.2 %reduce-scatter.13.cloned.1.call-start = ((), (), s32[]{:S(2)}) async-start(), calls=%async_computation.22 | async-start | bytes 33423360 | tf_op jit(solution)/shard_map/reduce_scatter | solution.py:375
  1148.6 980.0 %reduce-scatter.15.cloned.1.call-start = ((), (), s32[]{:S(2)}) async-start(), calls=%async_computation.23 | async-start | bytes 33423360 | tf_op jit(solution)/shard_map/reduce_scatter | solution.py:378
  1170.1 1257.0 %reduce-scatter.17.cloned.1.call-start = ((), (), s32[]{:S(2)}) async-start(), calls=%async_computation.24 | async-start | bytes 33423360 | tf_op jit(solution)/shard_map/reduce_scatter | solution.py:381
  1192.2 68.9 %copy-start.14 = (f32[256,1536]{1,0:T(8,128)S(1)}, f32[256,1536]{1,0:T(8,128)}, u32[]{:S(2)}) copy-start(f32[256,1536]{1,0:T(8,128)} %copy-done.13) | copy-start | bytes 4718596
  1192.2 68.9 %copy-start.26 = (bf16[256,1536]{1,0:T(8,128)(2,1)S(1)}, bf16[256,1536]{1,0:T(8,128)(2,1)}, u32[]{:S(2)}) copy-start(bf16[256,1536]{1,0:T(8,128)(2,1)} %param.25) | copy-start | bytes 2359300
  1192.2 73.0 %copy-start.64 = (f32[2,48]{1,0:T(2,128)S(1)}, f32[2,48]{1,0:T(2,128)}, u32[]{:S(2)}) copy-start(f32[2,48]{1,0:T(2,128)} %param.37) | copy-start | bytes 1156
  1192.2 73.0 %copy-start.65 = (f32[2,48]{1,0:T(2,128)S(1)}, f32[2,48]{1,0:T(2,128)}, u32[]{:S(2)}) copy-start(f32[2,48]{1,0:T(2,128)} %param.38) | copy-start | bytes 1156
  1192.3 162.4 %copy-start.34 = (f32[1536,48]{0,1:T(8,128)S(1)}, f32[1536,48]{0,1:T(8,128)}, u32[]{:S(2)}) copy-start(f32[1536,48]{0,1:T(8,128)} %param.33) | copy-start | bytes 884740
  1192.3 339.0 %copy-start.29 = (f32[48,2560]{1,0:T(8,128)S(1)}, f32[48,2560]{1,0:T(8,128)}, u32[]{:S(2)}) copy-start(f32[48,2560]{1,0:T(8,128)} %param.30) | copy-start | bytes 1474564
  1357.4 1156.5 %copy-start.37 = (f32[1536,48]{0,1:T(8,128)}, f32[1536,48]{0,1:T(8,128)S(1)}, u32[]{:S(2)}) copy-start(f32[1536,48]{0,1:T(8,128)S(1)} %get-tuple-element.184) | copy-start | bytes 884740
  1533.6 981.1 %copy-start.35 = (f32[48,2560]{1,0:T(8,128)}, f32[48,2560]{1,0:T(8,128)S(1)}, u32[]{:S(2)}) copy-start(f32[48,2560]{1,0:T(8,128)S(1)} %get-tuple-element.186) | copy-start | bytes 1474564
  1533.6 981.1 %copy-start.36 = (f32[48,2560]{1,0:T(8,128)}, f32[48,2560]{1,0:T(8,128)S(1)}, u32[]{:S(2)}) copy-start(f32[48,2560]{1,0:T(8,128)S(1)} %get-tuple-element.187) | copy-start | bytes 1474564
  (43 other events, 281.5 us)
Sparse Core Ops, SparseCore 0:
  11.5 78.2 all-gather.9
  93.3 66.0 all-gather.11
  161.5 160.5 all-gather.13
  324.1 158.1 all-gather.15
  484.3 158.1 all-gather.17
  1111.4 102.6 reduce-scatter.18
  1219.9 134.7 reduce-scatter.10
  1361.7 169.5 reduce-scatter.8
  1536.0 294.0 reduce-scatter.12
  1834.6 293.9 reduce-scatter.14
  2133.2 293.8 reduce-scatter.16
where the time goes:
time: 2530 us; the launch traced here: 2520 us
  waiting for transfers between devices  1640 us (65%)
  matrix products  284 us (11%)
  local copies, waits for them, and re-layouts  205 us (8%)
  blocking collectives  177 us (7%)
  other arithmetic  137 us (5%)
  starting transfers between devices  62.2 us (2%)
    reduce_scatter x1, waiting for transfers between devices, local(): lax.psum_scatter(gate_grad.astype(jnp.bfloat16), 'fsdp', scatter_dimensio...  296 us
    reduce_scatter x1, waiting for transfers between devices, local(): lax.psum_scatter(down_grad.astype(jnp.bfloat16), 'fsdp', scatter_dimensio...  289 us
    reduce_scatter x1, waiting for transfers between devices, local(): lax.psum_scatter(up_grad.astype(jnp.bfloat16), 'fsdp', scatter_dimension=...  289 us
    reduce_scatter x1, waiting for transfers between devices, local(): lax.psum_scatter(qkv_grad, ('fsdp', 'seq'), scatter_dimension=0, tiled=True)  174 us
    all_gather x1, waiting for transfers between devices, fetch_experts(): lax.all_gather(down_weight.astype(jnp.bfloat16), 'fsdp', axis=2, tiled=True)  141 us
    all_gather x1, waiting for transfers between devices, fetch_experts(): lax.all_gather(up_weight.astype(jnp.bfloat16), 'fsdp', axis=1, tiled=True)  89.3 us
    reduce_scatter x1, waiting for transfers between devices, local(): lax.psum_scatter(out_grad, ('fsdp', 'seq'), scatter_dimension=1, tiled=True)  88.8 us
    all_to_all x1, waiting for transfers between devices, local(): lax.all_to_all(grad_rows, 'seq', split_axis=0, concat_axis=0, tiled=True)  81 us
  transfers between devices with their start and end apart: 22, of which 14 were waited for; matrix products, arithmetic and copies ran while one was open for 15% of the time, Pallas kernels for 0%

commit v1 on v0

v1 whole, which is shorter than its diff:
```python
import functools

import jax
import jax.numpy as jnp
from jax import lax
from jax.experimental import pallas as pl
from jax.experimental.pallas import tpu as pltpu
from jax.sharding import PartitionSpec as P

D = 1536
NH = 24
KVH = 8
HD = 64
EXPERTS = 40
TOP = 8
STEP = 10
CAP = 76
FF = 512
TP = 4
SLOTS = 80
STEP_BLOCKS = 4
FLUSH = 4
MESH = pl.DeviceIdType.MESH


RESIDUAL_SCALE = 0.22
SCORE_SCALE = 0.015625
NORM_EPS = 1e-06
ROPE_BASE = 10000.0
CLIP_BASE = 4.5
BETA_ONE = 0.9
BETA_TWO = 0.999
ADAM_EPS = 1e-06
WEIGHT_DECAY = 0.01
LEARN_RATE = 0.3
MASK_FILL = -1e30


def rope_tables(positions, head_width):
    half_width = head_width // 2
    frequency = ROPE_BASE ** (-(jnp.arange(half_width, dtype=jnp.float32) * (2.0 / head_width)))
    angles = positions.astype(jnp.float32)[:, None] * frequency[None, :]
    return (jnp.cos(angles), jnp.sin(angles))


def rotate(values, cos_table, sin_table):
    half_width = values.shape[-1] // 2
    view_shape = (cos_table.shape[0],) + (1,) * (values.ndim - 2) + (half_width,)
    cos_view = cos_table.reshape(view_shape)
    sin_view = sin_table.reshape(view_shape)
    first_half = values[..., :half_width]
    second_half = values[..., half_width:]
    return jnp.concatenate(
        [
            first_half * cos_view - second_half * sin_view,
            second_half * cos_view + first_half * sin_view,
        ],
        axis=-1,
    )


def column_scale(factor):
    per_kv = NH // KVH
    head_part = jnp.repeat(factor.reshape(KVH, per_kv), HD, axis=1)
    return jnp.concatenate([head_part, jnp.ones((KVH, 2 * HD), factor.dtype)], axis=1).reshape(-1)


def adam_direction(weight_now, gradient, mean_old, square_old):
    momentum = BETA_ONE * mean_old + (1.0 - BETA_ONE) * gradient
    variance = BETA_TWO * square_old + (1.0 - BETA_TWO) * gradient * gradient
    direction = (
        momentum / (1.0 - BETA_ONE**STEP) / (jnp.sqrt(variance / (1.0 - BETA_TWO**STEP)) + ADAM_EPS)
        + WEIGHT_DECAY * weight_now
    )
    return (momentum, variance, direction)


def norm_back(values, inverse, gain, grad_normed):
    scaled = grad_normed * gain
    average = jnp.mean(scaled * values, axis=-1, keepdims=True)
    grad_values = inverse * (scaled - values * inverse * inverse * average)
    grad_gain = jnp.sum(grad_normed * values * inverse, axis=0)
    return (grad_values, grad_gain)


def shifted(array, by):
    devices = lax.axis_size("fsdp") * lax.axis_size("seq")
    pairs = [(i, i + by) for i in range(devices) if 0 <= i + by < devices]
    return lax.ppermute(array, ("fsdp", "seq"), pairs)


class Place:
    def __init__(self, same=False):
        fsdp = lax.axis_index("fsdp")
        self.line = fsdp // 4
        self.wide = (fsdp // 2) % 2
        self.core = fsdp % 2
        self.other = lax.axis_index("seq")
        self.turned = 0 if same else self.core

    def across(self, first, second):
        wide_step = first * (1 - self.turned) + second * self.turned
        other_step = first * self.turned + second * (1 - self.turned)
        wide = self.wide + wide_step * (1 - 2 * self.wide)
        other = self.other + other_step * (1 - 2 * self.other)
        return wide, other

    def device(self, line, wide, core, other):
        return (line * 4 + wide * 2 + core, other)

    def line_at(self, turn):
        if turn == 1:
            return self.line + 1 - 2 * (self.line % 2)
        if turn == 2:
            return self.line + 2 - 4 * (self.line // 2)
        return 3 - self.line if turn == 3 else self.line

    def peer_core(self):
        return self.device(self.line, self.wide, 1 - self.core, self.other)

    def peer_first(self):
        wide, other = self.across(1, 0)
        return self.device(self.line, wide, self.core, other)

    def peer_second(self):
        wide, other = self.across(0, 1)
        return self.device(self.line, wide, self.core, other)

    def peer_line(self, side):
        return self.device(self.line + 1 - 2 * side, self.wide, self.core, self.other)

    def goes_on(self, side):
        return self.line > 0 if side else self.line < 3

    def source(self, side, distance):
        line = self.line + distance if side else self.line - distance
        return line, (line <= 3 if side else line >= 0)

    def around(self, visit, nearest=0):
        if nearest == 0:
            visit(self.line)
        for distance in (1, 2, 3):
            for side in (0, 1):
                line, valid = self.source(side, distance)

                @pl.when(valid)
                def _():
                    visit(line)

    def peer_at(self, turn):
        return self.device(self.line_at(turn), self.wide, self.core, self.other)

    def peer_turned(self, turn):
        fsdp = lax.axis_index("fsdp") + turn
        return (fsdp % 16, self.other)

    def meet(self, everyone=False, whole_line=False):
        barrier = pltpu.get_barrier_semaphore()

        def greet(peer):
            pl.semaphore_signal(barrier, inc=1, device_id=peer, device_id_type=MESH)

        if everyone:
            for turn in range(1, 16):
                greet(self.peer_turned(turn))
            greet(self.device(self.line, self.wide, self.core, 1 - self.other))
            pl.semaphore_wait(barrier, 16)
            return
        for peer in (self.peer_core(), self.peer_first(), self.peer_second()):
            greet(peer)
        if whole_line:
            for turn in (1, 2, 3):
                greet(self.peer_at(turn))
            pl.semaphore_wait(barrier, 6)
            return
        for side in (0, 1):

            @pl.when(self.goes_on(side))
            def _():
                greet(self.peer_line(side))

        ends = (self.line == 0).astype(jnp.int32) + (self.line == 3).astype(jnp.int32)
        pl.semaphore_wait(barrier, 5 - ends)


def remote(source, target, send, recv, peer):
    return pltpu.make_async_remote_copy(
        src_ref=source,
        dst_ref=target,
        send_sem=send,
        recv_sem=recv,
        device_id=peer,
        device_id_type=MESH,
    )


class Gather:
    def __init__(self, place, src_ref, out_ref, sems):
        self.place, self.src, self.out = place, src_ref, out_ref
        (
            self.keep_sem, self.core_send, self.core_recv, self.line_send, self.line_recv,
            self.first_send, self.first_recv, self.second_send, self.second_recv,
        ) = sems
        width = src_ref.shape[1] // 2
        self.half = pl.ds(pl.multiple_of(place.core * width, 128), width)

    def unit(self, line, one, two):
        wide, other = self.place.across(one, two)
        return self.out.at[line, wide, :, other, :, self.half]

    def own(self):
        place = self.place
        return self.out.at[place.line, place.wide, place.core, place.other]

    def keep(self):
        return pltpu.make_async_copy(self.src, self.own(), self.keep_sem)

    def swap(self):
        at = self.place.line
        return remote(
            self.src, self.own(), self.core_send.at[at], self.core_recv.at[at], self.place.peer_core()
        )

    def to_core(self, line, one, two):
        ref = self.unit(line, one, two)
        at = (two * 2 + one) * 4 + line
        return remote(
            ref, ref, self.core_send.at[at], self.core_recv.at[at], self.place.peer_core()
        )

    def to_first(self, line):
        ref = self.unit(line, 0, 0)
        return remote(
            ref, ref, self.first_send.at[line], self.first_recv.at[line], self.place.peer_first()
        )

    def to_second(self, line, one):
        ref = self.unit(line, one, 0)
        at = one * 4 + line
        return remote(
            ref, ref, self.second_send.at[at], self.second_recv.at[at], self.place.peer_second()
        )

    def along(self, side, line):
        ref = self.unit(line, 0, 0)
        at = side * 4 + line
        return remote(
            ref, ref, self.line_send.at[at], self.line_recv.at[at], self.place.peer_line(side)
        )

    def begin(self):
        place = self.place
        self.keep().wait()
        self.swap().wait_recv()
        self.to_second(place.line, 0).start()
        self.to_first(place.line).start()
        for side in (0, 1):

            @pl.when(place.goes_on(side))
            def _():
                self.along(side, place.line).start()

    def at_distance(self, distance, visit):
        for side in (0, 1) if distance else (0,):
            line, valid = self.place.source(side, distance)
            pl.when(valid)(functools.partial(visit, side, line))

    def arrive(self, distance):
        def visit(side, line):
            self.along(side, line).wait_recv()
            self.to_second(line, 0).start()
            self.to_first(line).start()

            @pl.when(self.place.goes_on(side))
            def _():
                self.along(side, line).start()

            self.to_core(line, 0, 0).start()

        self.at_distance(distance, visit)

    def pass_first(self, distance):
        def visit(side, line):
            self.to_first(line).wait_recv()
            self.to_second(line, 1).start()
            self.to_core(line, 1, 0).start()

        self.at_distance(distance, visit)

    def pass_second(self, one, distance):
        def visit(side, line):
            self.to_second(line, one).wait_recv()
            self.to_core(line, one, 1).start()

        self.at_distance(distance, visit)

    def finish(self):
        def end_core(line, one, two):
            copy = self.to_core(line, one, two)
            copy.wait_recv()
            copy.wait_send()

        for distance in (1, 2, 3):
            self.at_distance(distance, lambda side, line: end_core(line, 0, 0))
        self.swap().wait_send()
        for line in range(4):
            for one, two in ((1, 0), (0, 1), (1, 1)):
                end_core(line, one, two)
            self.to_first(line).wait_send()
            for one in (0, 1):
                self.to_second(line, one).wait_send()
        for side in (0, 1):

            @pl.when(self.place.goes_on(side))
            def _():
                for distance in (0, 1, 2):
                    line, valid = self.place.source(side, distance)

                    @pl.when(valid)
                    def _():
                        self.along(side, line).wait_send()


class Spread:
    def __init__(self, place, src_ref, out_ref, sems, inner):
        self.place, self.src, self.out, self.inner = place, src_ref, out_ref, inner
        self.sends, self.recvs = sems

    def copy(self, turn):
        me = lax.axis_index("fsdp")
        target = self.out.at[:, me] if self.inner else self.out.at[me]
        peer = self.place.peer_turned(turn)
        source = self.src.at[peer[0]]
        if turn == 0:
            return pltpu.make_async_copy(source, target, self.sends.at[0])
        return remote(source, target, self.sends.at[turn], self.recvs.at[turn], peer)

    def begin(self):
        for turn in (8, 7, 9, 6, 10, 5, 11, 4, 12, 3, 13, 2, 14, 1, 15, 0):
            self.copy(turn).start()

    def finish(self):
        for turn in range(16):
            self.copy(turn).wait()


GATHER_SEMS = (0, 16, 16, 8, 8, 4, 4, 8, 8)


def gather_kernel(count, moves, *refs):
    place = Place()
    if moves:
        spread = Spread(place, refs[count], refs[2 * count + 1], refs[-2:], True)
        refs = refs[:count] + refs[count + 1 : 2 * count + 1] + refs[2 * count + 2 : -2]
    sems = refs[2 * count :]
    parts = [
        Gather(
            Place(same=moves and number == count - 1),
            refs[number],
            refs[count + number],
            sems[number * len(GATHER_SEMS) : (number + 1) * len(GATHER_SEMS)],
        )
        for number in range(count)
    ]
    for part in parts:
        part.keep().start()
    place.meet(moves)
    for part in parts:
        part.swap().start()
    for part in parts:
        part.begin()
    for distance in (1, 2, 3):
        for part in parts:
            part.arrive(distance)
        if moves and distance == 2:
            spread.begin()
        for part in parts:
            part.pass_first(distance - 1)
    for part in parts:
        part.pass_first(3)
    for one in (0, 1):
        for distance in range(4):
            for part in parts:
                part.pass_second(one, distance)
    for part in parts:
        part.finish()
    if moves:
        spread.finish()


def gather_all(number, *blocks, move=None):
    dma = pltpu.SemaphoreType.DMA
    size = sum(block.shape[0] * block.shape[1] for block in blocks)
    anywhere = pl.BlockSpec(memory_space=pl.ANY)
    shapes = [jax.ShapeDtypeStruct((4, 2, 2, 2) + block.shape, block.dtype) for block in blocks]
    scratch = [dma((many,)) if many else dma for many in GATHER_SEMS] * len(blocks)
    inputs = list(blocks)
    in_specs = [pl.BlockSpec(memory_space=pltpu.VMEM)] * len(blocks)
    if move is not None:
        inputs.append(move)
        in_specs.append(anywhere)
        shape = (move.shape[1], move.shape[0]) + move.shape[2:]
        shapes.append(jax.ShapeDtypeStruct(shape, move.dtype))
        scratch += [dma((16,)), dma((16,))]
    outs = pl.pallas_call(
        functools.partial(gather_kernel, len(blocks), move is not None),
        out_shape=shapes,
        in_specs=in_specs,
        out_specs=[anywhere] * len(shapes),
        scratch_shapes=scratch,
        compiler_params=pltpu.CompilerParams(collective_id=number, has_side_effects=True),
        cost_estimate=pl.CostEstimate(flops=0, bytes_accessed=128 * size, transcendentals=0),
    )(*inputs)
    full = [out.reshape((32,) + block.shape) for out, block in zip(outs, blocks)]
    return full + list(outs[len(blocks) :])


def devices_to(fn):
    pairs = []
    for number in range(32):
        fsdp, other = divmod(number, 2)
        line, wide, core, other = fn(fsdp // 4, (fsdp // 2) % 2, fsdp % 2, other)
        pairs.append((number, (line * 4 + wide * 2 + core) * 2 + other))
    return pairs


def permuted(array, fn):
    return lax.ppermute(array, ("fsdp", "seq"), devices_to(fn))


def swap_core(array):
    return permuted(array, lambda line, wide, core, other: (line, wide, 1 - core, other))


def swap_first(array):
    return permuted(
        array, lambda line, wide, core, other: (line, wide ^ (1 - core), core, other ^ core)
    )


def swap_second(array):
    return permuted(
        array, lambda line, wide, core, other: (line, wide ^ core, core, other ^ (1 - core))
    )


def swap_line(array, turn):
    return permuted(array, lambda line, wide, core, other: (line ^ turn, wide, core, other))


def add_kernel(left_ref, right_ref, anchor_ref, out_ref):
    total = left_ref[...].astype(jnp.float32) + right_ref[...].astype(jnp.float32)
    out_ref[...] = total.astype(out_ref.dtype)


def add_after(left, right, anchor):
    block = pl.BlockSpec((1,) + left.shape[1:], lambda i: (i,) + (0,) * (left.ndim - 1))
    return pl.pallas_call(
        add_kernel,
        grid=(left.shape[0],),
        out_shape=jax.ShapeDtypeStruct(left.shape, left.dtype),
        in_specs=[block, block, pl.BlockSpec(memory_space=pl.ANY)],
        out_specs=block,
        compiler_params=pltpu.CompilerParams(vmem_limit_bytes=32 * 1024 * 1024),
    )(left, right, anchor)


class Finish:
    def __init__(self, stay, leave):
        self.stay = stay
        self.there = swap_second(leave)

    def first(self, anchor):
        stay = add_after(self.stay, self.there, anchor)
        self.stay = stay[0]
        self.there = swap_first(stay[1])

    def column(self, anchor):
        return add_after(self.stay, self.there, anchor)


def sum_kernel(beside, ending, part_ref, *refs):
    if ending:
        column_ref, out_ref, mixture_ref = refs[:3]
        chips_ref, theirs_ref, got_ref, chips_load, chips_send, chips_recv, end_sems = refs[-7:]
        refs = (out_ref,) + refs[3:-7]
    if beside:
        mix_ref, grads_ref, out_ref, *mixed_refs, moved_ref = refs[:6]
        mix_core_ref, mix_own_ref, mix_load, mix_send, mix_recv, mix_store, *spread_sems = refs[-8:]
        refs = refs[6:-8]
    else:
        out_ref, *refs = refs
    (
        own_ref, core_ref, second_ref, first_ref, line_ref, last_ref,
        load_sem, core_send, core_recv, second_send, second_recv, first_send, first_recv,
        line_send, line_recv, last_send, last_recv,
    ) = refs
    place = Place()
    rows, columns = out_ref.shape
    width = columns // 2
    half = pl.ds(pl.multiple_of(place.core * width, 128), width)
    away = pl.ds(pl.multiple_of((1 - place.core) * width, 128), width)
    piece = 16 if rows % 64 else 64
    flip = place.line // 2
    low = place.line + flip * (3 - 2 * place.line)
    lines = [line + flip * (3 - 2 * line) for line in (3, 2 - 2 * low, 1 + low, low)]

    def slot(turn, one, two):
        return turn * 4 + two * 2 + one

    def unit(turn, one, two, where):
        wide, other = place.across(one, two)
        return part_ref.at[lines[turn], wide, :, other, :, where]

    def load(turn, one, two):
        at = slot(turn, one, two)
        return pltpu.make_async_copy(unit(turn, one, two, half), own_ref.at[at], load_sem.at[at])

    def swap(turn, one, two):
        at = slot(turn, two, one)
        return remote(
            unit(turn, one, two, away),
            core_ref.at[at],
            core_send.at[at],
            core_recv.at[at],
            place.peer_core(),
        )

    def to_second(turn, one):
        at = turn * 2 + one
        return remote(
            own_ref.at[slot(turn, one, 1)],
            second_ref.at[at],
            second_send.at[at],
            second_recv.at[at],
            place.peer_second(),
        )

    def to_first(turn):
        return remote(
            own_ref.at[slot(turn, 1, 0)],
            first_ref.at[turn],
            first_send.at[turn],
            first_recv.at[turn],
            place.peer_first(),
        )

    def along(side, turn):
        at = side * 4 + lines[turn]
        return remote(
            own_ref.at[slot(turn, 0, 0)],
            line_ref.at[at],
            line_send.at[at],
            line_recv.at[at],
            place.peer_line(side),
        )

    steps = ((1, 1), (0, 1), (1, 0), (0, 0))
    for turn in range(4):
        for one, two in steps:
            load(turn, one, two).start()
    place.meet(beside, ending)
    for turn in range(4):
        for two, one in steps:
            swap(turn, one, two).start()

    def chip(turn):
        if turn == 0:
            return pltpu.make_async_copy(column_ref.at[0], chips_ref.at[0], chips_load)
        return remote(
            column_ref.at[turn],
            chips_ref.at[turn],
            chips_send.at[turn],
            chips_recv.at[turn],
            place.peer_at(turn),
        )

    def end_mixture():
        count, width_end = theirs_ref.shape
        here = pl.ds(pl.multiple_of(place.core * width_end, 128), width_end)
        there = pl.ds(pl.multiple_of((1 - place.core) * width_end, 128), width_end)
        for turn in range(4):
            chip(turn).wait()

        def body(step, carry):
            at = pl.ds(pl.multiple_of(step * 64, 64), 64)
            for kind, core in enumerate((1 - place.core, place.core)):
                total = chips_ref[0, core, at, :].astype(jnp.float32)
                for turn in (1, 2, 3):
                    total += chips_ref[turn, core, at, :].astype(jnp.float32)
                if kind:
                    mixture_ref[at, here] = total
                else:
                    theirs_ref[at, :] = total.astype(theirs_ref.dtype)
            return carry

        lax.fori_loop(0, count // 64, body, 0)
        swap_end = remote(theirs_ref, got_ref, end_sems.at[0], end_sems.at[1], place.peer_core())
        swap_end.start()
        swap_end.wait()
        mixture_ref[:, there] = got_ref[...].astype(jnp.float32)

    if ending:
        for turn in (1, 2, 3, 0):
            chip(turn).start()
    if beside:
        spread = Spread(place, grads_ref, moved_ref, spread_sems, False)

    def mix_line(at):
        return place.line_at(at % 4)

    def mix_load_copy(at):
        wide, other = place.across(at // 4 % 2, at // 8)
        return pltpu.make_async_copy(
            mix_ref.at[mix_line(at), wide, :, other, :, half],
            mix_own_ref.at[at % 2],
            mix_load.at[at % 2],
        )

    def mix_give(at):
        wide, other = place.across(at // 8, at // 4 % 2)
        return remote(
            mix_ref.at[mix_line(at), wide, :, other, :, away],
            mix_core_ref.at[at],
            mix_send.at[at],
            mix_recv.at[at],
            place.peer_core(),
        )

    def mix_store_copy(at):
        return pltpu.make_async_copy(
            mix_core_ref.at[at], mixed_refs[at // 8].at[at // 4 % 2, at % 4], mix_store.at[at]
        )

    mix_order = [8 + at for at in range(8)] + [at for at in range(8)]

    def mix_begin():
        for at in mix_order:
            mix_give(at).start()
        for at in mix_order[:2]:
            mix_load_copy(at).start()

    def mix_add(number):
        at = mix_order[number]
        mix_load_copy(at).wait()
        mix_give(at).wait_recv()
        for core in range(2):

            def body(step, carry):
                here = pl.ds(pl.multiple_of(step * piece, 16), piece)
                total = mix_own_ref[at % 2, core, here, :].astype(jnp.float32)
                total += mix_core_ref[at, core, here, :].astype(jnp.float32)
                mix_core_ref[at, core, here, :] = total.astype(mix_core_ref.dtype)
                return carry

            lax.fori_loop(0, rows // piece, body, 0)
        mix_store_copy(at).start()
        if number + 2 < 16:
            mix_load_copy(mix_order[number + 2]).start()

    def add(at, others):
        for core in range(2):

            def body(step, carry):
                here = pl.ds(pl.multiple_of(step * piece, 16), piece)
                total = own_ref[at, core, here, :].astype(jnp.float32)
                for other in others:
                    total += other[core, here, :].astype(jnp.float32)
                own_ref[at, core, here, :] = total.astype(own_ref.dtype)
                return carry

            lax.fori_loop(0, rows // piece, body, 0)

    def ready(turn, one, two):
        load(turn, one, two).wait()
        swap(turn, two, one).wait_recv()
        return core_ref.at[slot(turn, one, two)]

    def give_second(turn):
        for one in (1, 0):
            add(slot(turn, one, 1), [ready(turn, one, 1)])
            to_second(turn, one).start()

    def give_first(turn):
        others = [ready(turn, 1, 0)]
        to_second(turn, 1).wait_recv()
        add(slot(turn, 1, 0), others + [second_ref.at[turn * 2 + 1]])
        to_first(turn).start()

    def take(side, turn):
        along(side, turn).wait_recv()
        add(slot(turn, 0, 0), [line_ref.at[side * 4 + lines[turn]]])

    def give_line(turn):
        others = [ready(turn, 0, 0)]
        to_second(turn, 0).wait_recv()
        to_first(turn).wait_recv()
        add(slot(turn, 0, 0), others + [second_ref.at[turn * 2], first_ref.at[turn]])
        for side in (0, 1):
            leaves = lines[turn] < place.line if side else lines[turn] > place.line
            arrives = place.goes_on(1 - side)
            if turn == 3:
                pl.when(arrives)(functools.partial(take, side, turn))
                continue

            @pl.when(leaves)
            def _():
                pl.when(arrives)(functools.partial(take, side, turn))
                along(side, turn).start()

    plan_steps = [
        functools.partial(give_second, 0),
        functools.partial(give_second, 1),
        functools.partial(give_second, 2),
        functools.partial(give_first, 0),
        functools.partial(give_second, 3),
        functools.partial(give_first, 1),
        functools.partial(give_line, 0),
        functools.partial(give_first, 2),
        functools.partial(give_line, 1),
        functools.partial(give_first, 3),
        functools.partial(give_line, 2),
    ]
    for number, step in enumerate(plan_steps):
        step()
        if beside and number == 0:
            mix_begin()
            spread.begin()
        if beside and number >= 3:
            mix_add(2 * number - 6)
            mix_add(2 * number - 5)
    give_line(3)
    if ending:
        end_mixture()
    mine = slot(3, 0, 0)
    last = remote(
        own_ref.at[mine, 1 - place.core], last_ref, last_send, last_recv, place.peer_core()
    )
    last.start()
    out_ref[:, half] = own_ref[mine, place.core].astype(out_ref.dtype)
    last.wait_recv()
    out_ref[:, away] = last_ref[...].astype(out_ref.dtype)
    last.wait_send()
    if beside:
        for at in range(16):
            mix_give(at).wait_send()
            mix_store_copy(at).wait()
        spread.finish()
    for turn in range(4):
        for one, two in steps:
            swap(turn, one, two).wait_send()
        to_second(turn, 0).wait_send()
        to_second(turn, 1).wait_send()
        to_first(turn).wait_send()
        if turn < 3:
            for side in (0, 1):
                leaves = lines[turn] < place.line if side else lines[turn] > place.line

                @pl.when(leaves)
                def _():
                    along(side, turn).wait_send()


def sum_all(part, number, mix=None, move=None, column=None):
    rows, columns = part.shape[0] // 32, part.shape[1]
    width = columns // 2
    dma = pltpu.SemaphoreType.DMA
    kind = part.dtype
    anywhere = pl.BlockSpec(memory_space=pl.ANY)
    inputs = [part.reshape(4, 2, 2, 2, rows, columns)]
    outs = [jax.ShapeDtypeStruct((rows, columns), kind)]
    out_specs = [pl.BlockSpec(memory_space=pltpu.VMEM)]
    sems = []
    if column is not None:
        inputs.append(column)
        count, width_end = column.shape[2:]
        outs.append(jax.ShapeDtypeStruct((count, 2 * width_end), jnp.float32))
        out_specs.append(pl.BlockSpec(memory_space=pltpu.VMEM))
        sems = [
            pltpu.VMEM(column.shape, kind),
            pltpu.VMEM((count, width_end), kind),
            pltpu.VMEM((count, width_end), kind),
            dma,
            dma((4,)),
            dma((4,)),
            dma((2,)),
        ]
    if mix is not None:
        inputs.append(mix.reshape(4, 2, 2, 2, rows, columns))
        inputs.append(move)
        outs += [jax.ShapeDtypeStruct((2, 4, 2, rows, width), kind)] * 2
        outs.append(jax.ShapeDtypeStruct(move.shape, move.dtype))
        out_specs += [anywhere] * 3
        sems = [
            pltpu.VMEM((16, 2, rows, width), kind),
            pltpu.VMEM((2, 2, rows, width), kind),
            dma((2,)),
            dma((16,)),
            dma((16,)),
            dma((16,)),
            dma((16,)),
            dma((16,)),
        ]
    return pl.pallas_call(
        functools.partial(sum_kernel, mix is not None, column is not None),
        out_shape=outs,
        in_specs=[anywhere] * len(inputs),
        out_specs=out_specs,
        scratch_shapes=[
            pltpu.VMEM((16, 2, rows, width), kind),
            pltpu.VMEM((16, 2, rows, width), kind),
            pltpu.VMEM((8, 2, rows, width), kind),
            pltpu.VMEM((4, 2, rows, width), kind),
            pltpu.VMEM((8, 2, rows, width), kind),
            pltpu.VMEM((rows, width), kind),
            dma((16,)),
            dma((16,)),
            dma((16,)),
            dma((8,)),
            dma((8,)),
            dma((4,)),
            dma((4,)),
            dma((8,)),
            dma((8,)),
            dma,
            dma,
        ]
        + sems,
        compiler_params=pltpu.CompilerParams(
            collective_id=number, has_side_effects=True, vmem_limit_bytes=60 * 1024 * 1024
        ),
        cost_estimate=pl.CostEstimate(
            flops=64 * rows * columns, bytes_accessed=128 * rows * columns, transcendentals=0
        ),
    )(*inputs)


def exchange_kernel(src_ref, out_ref, sends, recvs):
    place = Place()
    place.meet()
    line, wide, core, other = place.line, place.wide, place.core, place.other
    out_ref[line, wide, core, other] = src_ref[...]

    def along(side, at_line):
        ref = out_ref.at[at_line, wide, core, other]
        at = side * 4 + at_line
        return remote(ref, ref, sends.at[at], recvs.at[at], place.peer_line(side))

    def swap(ref, at, peer):
        copy = remote(ref, ref, sends.at[at], recvs.at[at], peer)
        copy.start()
        return copy

    for side in (0, 1):

        @pl.when(place.goes_on(side))
        def _():
            along(side, line).start()

    for distance in (1, 2, 3):
        for side in (0, 1):
            from_line, valid = place.source(side, distance)

            @pl.when(valid)
            def _():
                along(side, from_line).wait_recv()

                @pl.when(place.goes_on(side))
                def _():
                    along(side, from_line).start()

    for side in (0, 1):

        @pl.when(place.goes_on(side))
        def _():
            for distance in (0, 1, 2):
                from_line, valid = place.source(side, distance)

                @pl.when(valid)
                def _():
                    along(side, from_line).wait_send()

    swap(out_ref.at[:, wide, core, other], 8, place.device(line, 1 - wide, core, other)).wait()
    swap(out_ref.at[:, :, core, other], 9, place.device(line, wide, core, 1 - other)).wait()
    swap(out_ref.at[:, :, core], 10, place.peer_core()).wait()


def exchange_all(block, number):
    out = pl.pallas_call(
        exchange_kernel,
        out_shape=jax.ShapeDtypeStruct((4, 2, 2, 2) + block.shape, block.dtype),
        in_specs=[pl.BlockSpec(memory_space=pltpu.VMEM)],
        out_specs=pl.BlockSpec(memory_space=pltpu.VMEM),
        scratch_shapes=[pltpu.SemaphoreType.DMA((11,)), pltpu.SemaphoreType.DMA((11,))],
        compiler_params=pltpu.CompilerParams(collective_id=number, has_side_effects=True),
    )(block)
    return out.reshape((32,) + block.shape)


class Plan:
    def __init__(self):
        self.fsdp = lax.axis_size("fsdp")
        self.seq = lax.axis_size("seq")
        self.exp_dev = EXPERTS // self.seq
        self.units = self.exp_dev // (TP + 1)
        self.copies = self.fsdp // (TP * self.units)
        members = TP * self.units
        self.members = members
        self.near = [[c * members + i for i in range(members)] for c in range(self.copies)]
        self.far = [[c * members + i for c in range(self.copies)] for i in range(members)]
        self.blocks = members * self.seq
        self.plain = self.copies == 1
        self.direct = self.fsdp == 16 and self.seq == 2


def gather_attention(plan, qkv_weight, out_weight, norm_gains, routing, cots, packed):
    qkv_weight = qkv_weight.astype(jnp.bfloat16)
    out_weight = out_weight.astype(jnp.bfloat16)
    norm_gains = norm_gains.astype(jnp.bfloat16)
    if not plan.direct:
        return (
            lax.all_gather(qkv_weight, ("fsdp", "seq"), axis=0, tiled=True),
            lax.all_gather(out_weight, ("fsdp", "seq"), axis=0, tiled=True),
            lax.all_gather(norm_gains, ("fsdp", "seq"), axis=1, tiled=True),
            gather_tokens(plan, routing),
            gather_tokens(plan, cots).reshape(-1, D),
            send_weights(plan, packed),
        )
    rows, extra = qkv_weight.shape[0], routing.shape[1]
    wide_gains = jnp.pad(norm_gains, ((0, rows - 2 - routing.shape[0]), (0, extra - rows)))
    block = jnp.concatenate(
        [out_weight, jnp.concatenate([routing, wide_gains], axis=0)], axis=1
    )
    qkv_full, full, all_cots, weights = gather_all(0, qkv_weight, block, cots, move=packed)
    ends = out_weight.shape[1]
    at = routing.shape[0]
    return (
        qkv_full.reshape(D, -1),
        full[:, :, :ends].reshape(D, ends),
        jnp.transpose(full[:, at : at + 2, ends : ends + rows], (1, 0, 2)).reshape(2, D),
        full[:, :at, ends:],
        all_cots.reshape(-1, D),
        weights.reshape(3, D, weights.shape[3]),
    )


def sum_attention(plan, qkv_grad, out_grad, gains_grad, column):
    if not plan.direct:
        return (
            lax.psum_scatter(qkv_grad, ("fsdp", "seq"), scatter_dimension=0, tiled=True),
            lax.psum_scatter(out_grad, ("fsdp", "seq"), scatter_dimension=0, tiled=True),
            lax.psum_scatter(gains_grad, ("fsdp", "seq"), scatter_dimension=1, tiled=True),
            column,
        )
    split = qkv_grad.shape[1]
    ends = split + out_grad.shape[1]
    gains = jnp.pad(jnp.transpose(gains_grad), ((0, 0), (0, 254)))
    block = jnp.concatenate(
        [piece.astype(jnp.bfloat16) for piece in (qkv_grad, out_grad, gains)], axis=1
    )
    total, mixture = sum_all(block, 3, column=column)
    total = total.astype(jnp.float32)
    gains = jnp.transpose(total[:, ends : ends + 2])
    return total[:, :split], total[:, split:ends], gains, mixture


def gather_rows(plan, rows):
    if not plan.direct:
        return gather_tokens(plan, rows).reshape(-1, D)
    return gather_all(1, rows)[0].reshape(-1, D)


class Whole:
    def __init__(self, plan, part):
        self.total = scatter_tokens(plan, part)

    def first(self, anchor):
        pass

    def column(self, anchor):
        return self.total


def sum_rows(plan, back, mix, gate_grads, grads):
    gate_grads = return_grads(plan, gate_grads)
    if not plan.direct:
        return scatter_tokens(plan, back), Whole(plan, mix), gate_grads, return_grads(plan, grads)
    back, stay, leave, grads = sum_all(back, 2, mix=mix, move=grads)
    return back, Finish(stay, leave), gate_grads, grads


def share_stats(plan, stats):
    if not plan.direct:
        return lax.all_gather(stats, ("fsdp", "seq"), axis=0)
    block = jnp.pad(stats[None, :], ((0, 7), (0, 128 - stats.shape[0])))
    return exchange_all(block, 4)[:, 0, : stats.shape[0]]


def gather_tokens(plan, block):
    if plan.plain:
        return lax.all_gather(block, ("fsdp", "seq"), axis=0)
    block = lax.all_gather(block, "seq", axis=0)
    block = lax.all_gather(block, "fsdp", axis=0, axis_index_groups=plan.near)
    return block.reshape((plan.blocks,) + block.shape[2:])


def scatter_tokens(plan, partial):
    if plan.plain:
        return lax.psum_scatter(partial, ("fsdp", "seq"), scatter_dimension=0, tiled=True)
    partial = lax.psum_scatter(
        partial, "fsdp", scatter_dimension=0, tiled=True, axis_index_groups=plan.near
    )
    return lax.psum_scatter(partial, "seq", scatter_dimension=0, tiled=True)


def pack_kernel(gate_ref, up_ref, down_ref, out_ref):
    part = FF // TP
    for tensor, ref in enumerate((gate_ref, up_ref, down_ref)):
        for member in range(TP):
            out_ref[member, tensor, :, :FF] = ref[member].astype(jnp.bfloat16)
            out_ref[member, tensor, :, FF:] = ref[TP, :, member * part : (member + 1) * part].astype(
                jnp.bfloat16
            )


def pack_experts(plan, gate_weight, up_weight, down_weight):
    rows = gate_weight.shape[1]
    width = FF + FF // TP
    block = pl.BlockSpec((TP + 1, rows, FF), lambda i: (i, 0, 0))
    return pl.pallas_call(
        pack_kernel,
        grid=(plan.units,),
        out_shape=jax.ShapeDtypeStruct((plan.members, 3, rows, width), jnp.bfloat16),
        in_specs=[block] * 3,
        out_specs=pl.BlockSpec((TP, 3, rows, width), lambda i: (i, 0, 0, 0)),
        compiler_params=pltpu.CompilerParams(vmem_limit_bytes=32 * 1024 * 1024),
    )(gate_weight, up_weight, down_weight)


def lamb_kernel(*refs):
    weight_refs, first_refs, second_refs = refs[0:3], refs[3:6], refs[6:9]
    gates_ref, grads_ref = refs[9], refs[10]
    momentum_refs, variance_refs, direction_refs, sums_ref = refs[12:15], refs[15:18], refs[18:21], refs[21]
    part = FF // TP

    @pl.when(pl.program_id(0) == 0)
    def _():
        sums_ref[...] = jnp.zeros_like(sums_ref)

    for tensor in range(3):
        squares = [0.0, 0.0]
        for expert in range(TP + 1):
            def grad_of(member, columns):
                if tensor:
                    return grads_ref[member, tensor - 1, :, columns]
                return gates_ref[member, :, columns]

            if expert < TP:
                grad = grad_of(expert, slice(0, FF))
            else:
                grad = jnp.concatenate(
                    [grad_of(member, slice(FF, FF + part)) for member in range(TP)], axis=1
                )
            weight = weight_refs[tensor][expert]
            momentum, variance, direction = adam_direction(
                weight,
                grad.astype(jnp.float32),
                first_refs[tensor][expert],
                second_refs[tensor][expert],
            )
            momentum_refs[tensor][expert] = momentum
            variance_refs[tensor][expert] = variance
            direction_refs[tensor][expert] = direction
            squares[0] += weight * weight
            squares[1] += direction * direction
        for kind in range(2):
            rows = squares[kind].reshape(-1, 8, FF)
            total = jnp.sum(rows, axis=0)
            for lane in range(0, FF, 128):
                sums_ref[2 * tensor + kind] += total[:, lane : lane + 128]


def lamb_experts(plan, weights, firsts, seconds, gates, packed, anchor):
    rows = weights[0].shape[1]
    shape = jax.ShapeDtypeStruct(weights[0].shape, jnp.float32)
    block = pl.BlockSpec((TP + 1, rows, FF), lambda i: (i, 0, 0))
    outs = pl.pallas_call(
        lamb_kernel,
        grid=(plan.units,),
        out_shape=[shape] * 9 + [jax.ShapeDtypeStruct((8, 8, 128), jnp.float32)],
        in_specs=[block] * 9
        + [
            pl.BlockSpec((TP, rows, packed.shape[3]), lambda i: (i, 0, 0)),
            pl.BlockSpec((TP, 2, rows, packed.shape[3]), lambda i: (i, 0, 0, 0)),
            pl.BlockSpec(memory_space=pl.ANY),
        ],
        out_specs=[block] * 9 + [pl.BlockSpec((8, 8, 128), lambda i: (0, 0, 0))],
        compiler_params=pltpu.CompilerParams(vmem_limit_bytes=56 * 1024 * 1024),
        cost_estimate=pl.CostEstimate(
            flops=60 * weights[0].size,
            bytes_accessed=80 * weights[0].size,
            transcendentals=6 * weights[0].size,
        ),
    )(*weights, *firsts, *seconds, gates, packed, anchor)
    sums = jnp.sum(outs[9], axis=(1, 2))
    return list(zip(outs[0:3], outs[3:6], outs[6:9])), sums[0:6:2], sums[1:6:2]


def send_weights(plan, packed):
    if plan.copies == 1:
        got = lax.all_to_all(packed, "fsdp", split_axis=0, concat_axis=0, tiled=True)
    else:
        got = lax.all_to_all(
            packed, "fsdp", split_axis=0, concat_axis=0, tiled=True, axis_index_groups=plan.near
        )
        got = lax.all_gather(got, "fsdp", axis=0, tiled=True, axis_index_groups=plan.far)
    return jnp.transpose(got, (1, 0, 2, 3)).reshape(3, D, got.shape[3])


def return_grads(plan, blocks):
    if plan.copies > 1:
        blocks = lax.psum_scatter(
            blocks, "fsdp", scatter_dimension=0, tiled=True, axis_index_groups=plan.far
        )
        return lax.all_to_all(
            blocks, "fsdp", split_axis=0, concat_axis=0, tiled=True, axis_index_groups=plan.near
        )
    return lax.all_to_all(blocks, "fsdp", split_axis=0, concat_axis=0, tiled=True)


def route_table(plan, packed, experts):
    routed = packed[:, :TOP]
    gates = packed[:, TOP:].astype(jnp.float32)
    tokens = packed.shape[-1]
    earlier = (
        jnp.arange(tokens, dtype=jnp.int32)[:, None] <= jnp.arange(tokens, dtype=jnp.int32)[None, :]
    ).astype(jnp.bfloat16)
    ranks = []
    weights = []
    for expert in experts:
        match = routed == expert.astype(jnp.bfloat16)
        here = jnp.any(match, axis=1)
        order = jnp.dot(
            here.astype(jnp.bfloat16), earlier, preferred_element_type=jnp.float32
        )
        ranks.append(jnp.where(here, order - 1.0, -1.0))
        weights.append(jnp.sum(jnp.where(match, gates, 0.0), axis=1))
    filler = jnp.zeros_like(ranks[0])
    return jnp.stack(ranks + weights + [filler] * 4, axis=1)


NATURAL = (((1,), (0,)), ((), ()))
RIGHT_TURNED = (((1,), (1,)), ((), ()))
LEFT_TURNED = (((0,), (0,)), ((), ()))


def product(left, right, dims=NATURAL):
    return lax.dot_general(left, right, dims, preferred_element_type=jnp.float32)


def expert_kernel(
    steps, tokens, table_ref, rows_ref, cots_ref, weights_ref, out_ref, back_ref, gates_ref,
    grads_ref, total_ref, picked_ref, pulled_ref, result_ref, return_ref,
):
    step = pl.program_id(0)
    grad_rows = grads_ref.shape[2]

    @pl.when(step == 0)
    def _():
        total_ref[...] = jnp.zeros_like(total_ref)

    @pl.when(step < steps)
    def _():
        slot_of = lax.broadcasted_iota(jnp.int32, (SLOTS, tokens), 0).astype(jnp.float32)

        def spread_table(block, first):
            chosen = [slot_of == table_ref[block, unit : unit + 1, :] for unit in range(2)]
            if first is None:
                return jnp.concatenate([jnp.where(one, 1.0, 0.0) for one in chosen], axis=0)
            return jnp.concatenate(
                [
                    jnp.where(one, table_ref[block, first + unit : first + unit + 1, :], 0.0)
                    for unit, one in enumerate(chosen)
                ],
                axis=0,
            )

        for block in range(STEP_BLOCKS):
            hot = spread_table(block, None).astype(jnp.bfloat16)
            gate = jnp.sum(spread_table(block, 2), axis=1, keepdims=True)
            own = pl.ds(block * tokens, tokens)
            place = pl.ds(block * SLOTS, SLOTS)
            picked = product(hot, rows_ref[own, :]).astype(jnp.bfloat16)
            pulled = (RESIDUAL_SCALE * gate * product(hot, cots_ref[own, :])).astype(jnp.bfloat16)
            for unit in range(2):
                half = slice(unit * SLOTS, (unit + 1) * SLOTS)
                picked_ref[unit, place, :] = picked[half]
                pulled_ref[unit, place, :] = pulled[half]
        for unit, columns in ((0, pl.ds(0, FF)), (1, pl.ds(FF, FF // TP))):
            rows = picked_ref[unit]
            cots = pulled_ref[unit]
            gate_weight = weights_ref[0, :, columns]
            up_weight = weights_ref[1, :, columns]
            down_weight = weights_ref[2, :, columns]
            gate_pre = product(rows, gate_weight)
            up_pre = product(rows, up_weight)
            grad_act = product(cots, down_weight)
            sigmoid_gate = jax.nn.sigmoid(gate_pre)
            activated = gate_pre * sigmoid_gate
            hidden_act = (activated * up_pre).astype(jnp.bfloat16)
            slope = sigmoid_gate * (1.0 + gate_pre * (1.0 - sigmoid_gate))
            grad_gate = (grad_act * up_pre * slope).astype(jnp.bfloat16)
            grad_up = (grad_act * activated).astype(jnp.bfloat16)
            result_ref[unit] = product(hidden_act, down_weight, RIGHT_TURNED).astype(jnp.bfloat16)
            return_ref[unit] = (
                product(grad_gate, gate_weight, RIGHT_TURNED)
                + product(grad_up, up_weight, RIGHT_TURNED)
            ).astype(jnp.bfloat16)
            total_ref[0, :, columns] += product(rows, grad_gate, LEFT_TURNED)
            total_ref[1, :, columns] += product(rows, grad_up, LEFT_TURNED)
            total_ref[2, :, columns] += product(cots, hidden_act, LEFT_TURNED)
        for block in range(STEP_BLOCKS):
            own = pl.ds(block * tokens, tokens)
            place = pl.ds(block * SLOTS, SLOTS)

            def both(ref):
                return jnp.concatenate([ref[0, place, :], ref[1, place, :]], axis=0)

            hot = spread_table(block, None).astype(jnp.bfloat16)
            gated = spread_table(block, 2).astype(jnp.bfloat16)
            out_ref[own, :] = product(gated, both(result_ref), LEFT_TURNED).astype(jnp.bfloat16)
            back_ref[own, :] = product(hot, both(return_ref), LEFT_TURNED).astype(jnp.bfloat16)

    @pl.when(step >= steps)
    def _():
        per_step = grads_ref.shape[0]
        for piece in range(per_step):
            first = pl.multiple_of(((step - steps) * per_step + piece) * grad_rows, 16)
            for tensor in range(3):
                grad = total_ref[tensor, pl.ds(first, grad_rows), :].astype(jnp.bfloat16)
                if tensor:
                    grads_ref[piece, tensor - 1] = grad
                else:
                    gates_ref[piece] = grad


def run_experts(table, rows, cots, weights, owners):
    blocks, _, tokens = table.shape
    steps = blocks // STEP_BLOCKS
    width = weights.shape[2]
    grad_rows = D // owners
    last = steps - 1
    chunk = STEP_BLOCKS * tokens
    stream = pl.BlockSpec((chunk, D), lambda i: (jnp.minimum(i, last), 0))
    slots = STEP_BLOCKS * SLOTS
    return pl.pallas_call(
        functools.partial(expert_kernel, steps, tokens),
        grid=(steps + FLUSH,),
        out_shape=(
            jax.ShapeDtypeStruct((blocks * tokens, D), jnp.bfloat16),
            jax.ShapeDtypeStruct((blocks * tokens, D), jnp.bfloat16),
            jax.ShapeDtypeStruct((owners, grad_rows, width), jnp.bfloat16),
            jax.ShapeDtypeStruct((owners, 2, grad_rows, width), jnp.bfloat16),
        ),
        in_specs=[
            pl.BlockSpec((STEP_BLOCKS, 8, tokens), lambda i: (jnp.minimum(i, last), 0, 0)),
            stream,
            stream,
            pl.BlockSpec((3, D, width), lambda i: (0, 0, 0), pipeline_mode=pl.Buffered(1)),
        ],
        out_specs=(
            stream,
            stream,
            pl.BlockSpec(
                (owners // FLUSH, grad_rows, width), lambda i: (jnp.maximum(i - steps, 0), 0, 0)
            ),
            pl.BlockSpec(
                (owners // FLUSH, 2, grad_rows, width),
                lambda i: (jnp.maximum(i - steps, 0), 0, 0, 0),
            ),
        ),
        scratch_shapes=[
            pltpu.VMEM((3, D, width), jnp.float32),
            pltpu.VMEM((2, slots, D), jnp.bfloat16),
            pltpu.VMEM((2, slots, D), jnp.bfloat16),
            pltpu.VMEM((2, slots, D), jnp.bfloat16),
            pltpu.VMEM((2, slots, D), jnp.bfloat16),
        ],
        compiler_params=pltpu.CompilerParams(vmem_limit_bytes=62 * 1024 * 1024),
        cost_estimate=pl.CostEstimate(
            flops=blocks * SLOTS * 2 * D * (9 * width + 8 * tokens),
            bytes_accessed=blocks * tokens * D * 8 + 3 * D * width * 4,
            transcendentals=blocks * SLOTS * width,
        ),
    )(table, rows, cots, weights)


def local(
    hidden_in,
    grad_out,
    routes,
    gate_weights,
    doc_start,
    qkv_weight,
    qkv_first,
    qkv_second,
    out_weight,
    out_first,
    out_second,
    norm_gains,
    gains_first,
    gains_second,
    gate_weight,
    gate_first,
    gate_second,
    up_weight,
    up_first,
    up_second,
    down_weight,
    down_first,
    down_second,
):
    plan = Plan()
    seq_index = lax.axis_index("seq")
    fsdp_index = lax.axis_index("fsdp")
    seq_count = plan.seq
    tok_rows = hidden_in.shape[0]
    per_kv = NH // KVH
    group_width = (per_kv + 2) * HD
    out_weight, out_first, out_second = (jnp.transpose(a) for a in (out_weight, out_first, out_second))
    down_weight, down_first, down_second = (
        jnp.transpose(a, (0, 2, 1)) for a in (down_weight, down_first, down_second)
    )

    qkv_full, out_full, gains_full, all_routes, all_cots, expert_weights = gather_attention(
        plan,
        qkv_weight,
        out_weight,
        norm_gains,
        jnp.concatenate([jnp.transpose(routes).astype(jnp.bfloat16), jnp.transpose(gate_weights)]),
        grad_out,
        pack_experts(plan, gate_weight, up_weight, down_weight),
    )
    member = lax.rem(fsdp_index, plan.members)
    first_expert = seq_index * plan.exp_dev + (member // TP) * (TP + 1)
    table = route_table(plan, all_routes, (first_expert + lax.rem(member, TP), first_expert + TP))

    attn_gain = gains_full[0].astype(jnp.float32)
    ffn_gain = gains_full[1].astype(jnp.float32)
    hidden = hidden_in.astype(jnp.float32)
    inverse_one = lax.rsqrt(jnp.mean(hidden * hidden, axis=-1, keepdims=True) + NORM_EPS)
    normed_one = (hidden * inverse_one * attn_gain).astype(jnp.bfloat16)
    projected = jnp.dot(normed_one, qkv_full, preferred_element_type=jnp.float32).reshape(
        tok_rows, KVH, group_width
    )
    first_token = (fsdp_index * seq_count + seq_index) * tok_rows
    token_pos = first_token + jnp.arange(tok_rows, dtype=jnp.int32)
    own_starts = lax.dynamic_slice_in_dim(doc_start, seq_index * tok_rows, tok_rows)
    cos_table, sin_table = rope_tables(token_pos - own_starts, HD)
    turned = rotate(
        projected[:, :, : (per_kv + 1) * HD].reshape(tok_rows, KVH, per_kv + 1, HD),
        cos_table,
        sin_table,
    ).astype(jnp.bfloat16)
    queries = turned[:, :, :per_kv]
    keyvals = jnp.concatenate(
        [turned[:, :, per_kv], projected[:, :, (per_kv + 1) * HD :].astype(jnp.bfloat16)], axis=-1
    )
    both_kv = jnp.concatenate(
        [shifted(keyvals, by) for by in range(seq_count, 0, -1)] + [keyvals], axis=0
    )
    keys_all = both_kv[:, :, :HD]
    values_all = both_kv[:, :, HD:]
    key_count = (seq_count + 1) * tok_rows
    key_pos = first_token - seq_count * tok_rows + jnp.arange(key_count, dtype=jnp.int32)
    allowed = (key_pos[None, :] >= own_starts[:, None]) & (key_pos[None, :] <= token_pos[:, None])
    scores = (
        jnp.einsum("qjid,kjd->jiqk", queries, keys_all, preferred_element_type=jnp.float32)
        * SCORE_SCALE
    )
    masked = jnp.where(allowed, scores, MASK_FILL)
    row_peak = jnp.max(masked, axis=-1, keepdims=True)
    exponent = jnp.where(allowed, jnp.exp(masked - row_peak), 0.0)
    row_total = jnp.sum(exponent, axis=-1, keepdims=True)
    attn_probs = exponent / row_total
    rounded = attn_probs.astype(jnp.bfloat16)
    attn_tokens = (
        jnp.einsum("jiqk,kjd->qjid", rounded, values_all, preferred_element_type=jnp.float32)
        .astype(jnp.bfloat16)
        .reshape(tok_rows, NH * HD)
    )
    head_peak = jnp.max(row_peak, axis=(2, 3)).reshape(NH)

    after_attn = hidden + RESIDUAL_SCALE * lax.dot_general(
        attn_tokens, out_full, RIGHT_TURNED, preferred_element_type=jnp.float32
    )
    inverse_two = lax.rsqrt(jnp.mean(after_attn * after_attn, axis=-1, keepdims=True) + NORM_EPS)
    normed_two = (after_attn * inverse_two * ffn_gain).astype(jnp.bfloat16)
    all_rows = gather_rows(plan, normed_two)
    mix_part, back_part, gate_grads, expert_grads = run_experts(
        table, all_rows, all_cots, expert_weights, plan.fsdp
    )
    back_sum, mix_sum, own_gates, own_grads = sum_rows(
        plan, back_part, mix_part, gate_grads, expert_grads
    )
    grad_normed_two = back_sum.astype(jnp.float32)
    back_two, gain_grad_two = norm_back(after_attn, inverse_two, ffn_gain, grad_normed_two)
    grad_after = grad_out.astype(jnp.float32) + back_two
    grad_attn = (RESIDUAL_SCALE * grad_after).astype(jnp.bfloat16)
    out_grad = jnp.einsum("tc,td->dc", attn_tokens, grad_attn, preferred_element_type=jnp.float32)
    grad_mixed = (
        jnp.dot(grad_attn, out_full, preferred_element_type=jnp.float32)
        .astype(jnp.bfloat16)
        .reshape(tok_rows, KVH, per_kv, HD)
    )
    grad_probs = jnp.einsum(
        "qjid,kjd->jiqk", grad_mixed, values_all, preferred_element_type=jnp.float32
    )
    centre = jnp.sum(attn_probs * grad_probs, axis=-1, keepdims=True)
    grad_scores = (attn_probs * (grad_probs - centre)).astype(jnp.bfloat16)
    grad_query = (
        jnp.einsum("jiqk,kjd->qjid", grad_scores, keys_all, preferred_element_type=jnp.float32)
        * SCORE_SCALE
    )
    grad_key = (
        jnp.einsum("jiqk,qjid->kjd", grad_scores, queries, preferred_element_type=jnp.float32)
        * SCORE_SCALE
    )
    grad_value = jnp.einsum(
        "jiqk,qjid->kjd", rounded, grad_mixed, preferred_element_type=jnp.float32
    )
    grad_kv = jnp.concatenate([grad_key, grad_value], axis=-1)
    mix_sum.first(grad_query[:8, 0, 0])
    own_kv = grad_kv[seq_count * tok_rows :]
    for by in range(seq_count, 0, -1):
        piece = grad_kv[(seq_count - by) * tok_rows : (seq_count - by + 1) * tok_rows]
        own_kv = own_kv + shifted(piece.astype(jnp.bfloat16), -by).astype(jnp.float32)
    query_key = jnp.concatenate([grad_query, own_kv[:, :, None, :HD]], axis=2)
    unturned = rotate(query_key, cos_table, -sin_table).reshape(tok_rows, KVH, (per_kv + 1) * HD)
    grad_projected = (
        jnp.concatenate([unturned, own_kv[:, :, HD:]], axis=2)
        .astype(jnp.bfloat16)
        .reshape(tok_rows, KVH * group_width)
    )
    qkv_grad = jnp.einsum(
        "tc,tq->cq", normed_one, grad_projected, preferred_element_type=jnp.float32
    )
    grad_normed_one = jnp.einsum(
        "tq,cq->tc", grad_projected, qkv_full, preferred_element_type=jnp.float32
    )
    back_one, gain_grad_one = norm_back(hidden, inverse_one, attn_gain, grad_normed_one)
    input_grad = grad_after + back_one
    gains_grad = jnp.stack([gain_grad_one, gain_grad_two])
    summed_qkv, summed_out, summed_gains, mixture = sum_attention(
        plan, qkv_grad, out_grad, gains_grad, mix_sum.column(grad_projected[:8, :128])
    )
    block_output = (after_attn + RESIDUAL_SCALE * mixture.astype(jnp.float32)).astype(jnp.bfloat16)
    weight_list = [
        qkv_weight,
        out_weight,
        norm_gains[0],
        norm_gains[1],
        gate_weight,
        up_weight,
        down_weight,
    ]
    grad_list = [summed_qkv, summed_out, summed_gains[0], summed_gains[1]]
    mean_list = [qkv_first, out_first, gains_first[0], gains_first[1]]
    square_list = [qkv_second, out_second, gains_second[0], gains_second[1]]
    updates = [
        adam_direction(weight_now, gradient, mean_old, square_old)
        for weight_now, gradient, mean_old, square_old in zip(
            weight_list[:4], grad_list, mean_list, square_list
        )
    ]
    expert_updates, expert_weight, expert_step = lamb_experts(
        plan,
        weight_list[4:],
        [gate_first, up_first, down_first],
        [gate_second, up_second, down_second],
        own_gates,
        own_grads,
        grad_query[:8, 0, 0],
    )
    local_weight = jnp.concatenate(
        [
            jnp.stack([jnp.sum(weight_now * weight_now) for weight_now in weight_list[:4]]),
            expert_weight,
        ]
    )
    local_step = jnp.concatenate(
        [jnp.stack([jnp.sum(piece[2] * piece[2]) for piece in updates]), expert_step]
    )
    updates += expert_updates
    stats = share_stats(plan, jnp.concatenate([local_weight, local_step, head_peak]))
    weight_norm = jnp.sqrt(jnp.sum(stats[:, :7], axis=0))
    step_norm = jnp.sqrt(jnp.sum(stats[:, 7:14], axis=0))
    peak_heads = jnp.max(stats[:, 14:], axis=0)
    trust_ratio = weight_norm / step_norm
    masters = [
        weight_list[number] - LEARN_RATE * trust_ratio[number] * updates[number][2]
        for number in range(7)
    ]
    clip_limit = CLIP_BASE * HD**0.5 / 8.0
    clip_factors = clip_limit / jnp.maximum(peak_heads, clip_limit)
    qkv_master = masters[0] * column_scale(clip_factors)[None, :]
    return (
        block_output,
        input_grad,
        qkv_master,
        updates[0][0],
        updates[0][1],
        jnp.transpose(masters[1]),
        jnp.transpose(updates[1][0]),
        jnp.transpose(updates[1][1]),
        jnp.stack([masters[2], masters[3]]),
        jnp.stack([updates[2][0], updates[3][0]]),
        jnp.stack([updates[2][1], updates[3][1]]),
        masters[4],
        updates[4][0],
        updates[4][1],
        masters[5],
        updates[5][0],
        updates[5][1],
        jnp.transpose(masters[6], (0, 2, 1)),
        jnp.transpose(updates[6][0], (0, 2, 1)),
        jnp.transpose(updates[6][1], (0, 2, 1)),
        clip_factors,
        jnp.stack([weight_norm, step_norm]),
    )


def solution(mesh):
    return jax.shard_map(
        local,
        mesh=mesh,
        in_specs=(
            P(("fsdp", "seq"), None),
            P(("fsdp", "seq"), None),
            P(("fsdp", "seq"), None),
            P(("fsdp", "seq"), None),
            P("fsdp"),
            P(("fsdp", "seq"), None),
            P(("fsdp", "seq"), None),
            P(("fsdp", "seq"), None),
            P(None, ("fsdp", "seq")),
            P(None, ("fsdp", "seq")),
            P(None, ("fsdp", "seq")),
            P(None, ("fsdp", "seq")),
            P(None, ("fsdp", "seq")),
            P(None, ("fsdp", "seq")),
            P("seq", "fsdp", None),
            P("seq", "fsdp", None),
            P("seq", "fsdp", None),
            P("seq", "fsdp", None),
            P("seq", "fsdp", None),
            P("seq", "fsdp", None),
            P("seq", None, "fsdp"),
            P("seq", None, "fsdp"),
            P("seq", None, "fsdp"),
        ),
        out_specs=(
            P(("fsdp", "seq"), None),
            P(("fsdp", "seq"), None),
            P(("fsdp", "seq"), None),
            P(("fsdp", "seq"), None),
            P(("fsdp", "seq"), None),
            P(None, ("fsdp", "seq")),
            P(None, ("fsdp", "seq")),
            P(None, ("fsdp", "seq")),
            P(None, ("fsdp", "seq")),
            P(None, ("fsdp", "seq")),
            P(None, ("fsdp", "seq")),
            P("seq", "fsdp", None),
            P("seq", "fsdp", None),
            P("seq", "fsdp", None),
            P("seq", "fsdp", None),
            P("seq", "fsdp", None),
            P("seq", "fsdp", None),
            P("seq", None, "fsdp"),
            P("seq", None, "fsdp"),
            P("seq", None, "fsdp"),
            P(),
            P(),
        ),
        check_vma=False,
    )
```

time: 2530 us -> 1020 us (0.40)
  waiting for transfers between devices: 1640 us -> 27.5 us
  Pallas kernels: 0 us -> 723 us
  matrix products: 284 us -> 83.5 us
  blocking collectives: 177 us -> 0 us
  local copies, waits for them, and re-layouts: 205 us -> 66 us
  other arithmetic: 137 us -> 84.4 us
  starting transfers between devices: 62.2 us -> 16.2 us
    reduce_scatter x5 -> x0, waiting for transfers between devices: 1140 us -> none  [the longest x1 296 us: local(): lax.psum_scatter(gate_grad.astype(jnp.bfloat16), 'fsdp', scatter_dimensio...]
    pallas_call x0 -> x10, Pallas kernels: none -> 723 us  [the longest x2 317 us: gather_all(): pl.pallas_call(functools.partial(gather_kernel, len(blocks), move is not...]
    all_to_all x9 -> x1, waiting for transfers between devices: 270 us -> 0.01 us  [return_grads(): lax.all_to_all(blocks, 'fsdp', split_axis=0, concat_axis=0, tiled=True)]
    all_gather x5 -> x0, waiting for transfers between devices: 230 us -> none  [the longest x1 141 us: fetch_experts(): lax.all_gather(down_weight.astype(jnp.bfloat16), 'fsdp', axis=2, tiled=True)]
    dot_general x18 -> x11, matrix products: 261 us -> 54.5 us  [the longest x1 12.1 us: local(): jnp.einsum('qjid,kjd->jiqk', grad_mixed, values_all, preferred_element_ty...]
    all_gather x2 -> x0, blocking collectives: 137 us -> none  [the longest x1 69.6 us: local(): lax.all_gather(norm_gains.astype(jnp.bfloat16), ('fsdp', 'seq'), axis=1,...]
    gather x5 -> x0, local copies, waits for them, and re-layouts: 85.3 us -> none  [the longest x1 19.4 us: local(): jnp.concatenate([gate_weights.reshape(-1), jnp.zeros((1,), jnp.bfloat16)])]
    all_to_all x9 -> x1, starting transfers between devices: 58.2 us -> 4.43 us  [return_grads(): lax.all_to_all(blocks, 'fsdp', split_axis=0, concat_axis=0, tiled=True)]
  transfers between devices with their start and end apart: 22 -> 7, of which waited for: 14 -> 1; matrix products, arithmetic and copies ran while one was open for 15% -> 11% of each run, Pallas kernels for 0% -> 3%
where the time goes in v1:
time: 1020 us; the launch traced here: 1010 us
  Pallas kernels  723 us (71%)
  other arithmetic  84.4 us (8%)
  matrix products  83.5 us (8%)
  local copies, waits for them, and re-layouts  66 us (6%)
  waiting for transfers between devices  27.5 us (3%)
  starting transfers between devices  16.2 us (2%)
    pallas_call x2, Pallas kernels, gather_all(): pl.pallas_call(functools.partial(gather_kernel, len(blocks), move is not...  317 us
    pallas_call x2, Pallas kernels, sum_all(): pl.pallas_call(functools.partial(sum_kernel, mix is not None, column is n...  253 us
    pallas_call x1, Pallas kernels, run_experts(): pl.pallas_call(functools.partial(expert_kernel, steps, tokens), grid=(ste...  101 us
    ppermute x4, waiting for transfers between devices, shifted(): return lax.ppermute(array, ('fsdp', 'seq'), pairs)  27.5 us
    pallas_call x1, Pallas kernels, lamb_experts(): pl.pallas_call(lamb_kernel, grid=(plan.units,), out_shape=[shape] * 9 + [...  27.1 us
    unnamed x134, local copies, waits for them, and re-layouts  24.4 us
  transfers between devices with their start and end apart: 7, of which 1 were waited for; matrix products, arithmetic and copies ran while one was open for 11% of the time, Pallas kernels for 3%

profile of v1, /device:TPU:0, one launch (start us, length us, event | category | flops | bytes accessed | tf_op | source)
XLA Modules:
  0.0 1006.9 jit_solution(6981700443893359670)
XLA Ops:
  6.2 2.1 copy-done
  8.3 2.1 copy-done.1
  10.4 2.1 copy-done.3
  13.2 2.6 copy-done.5
  16.5 204.5 %shard_map.391 = (bf16[4,2,2,2,48,2560]{5,4,3,2,1,0:T(8,128)(2,1)}, bf16[4,2,2,2,48,1792]{5,4,3,2,1,0:T(8,128)(2,1)}, bf16[4,2,2,2,256,1536]{5,4,3,2,1,0:T(8,128)(2,1)}, bf16[3,16,96,640]{3,2,1,0:T(8,128)(2,1)}) custom-call(bf16[48,2560]{1,0:T(8,128)(2,1)} %convert_element_type.127.refs_0_, bf16[48,1792]{1,0:T(8,128)(2,1)} %fusion.65.refs_1_, ...), custom_call_target="tpu_custom_call" | custom-call | bytes 77070336 | tf_op jit(solution)/shard_map/pallas_call | solution.py:405
  222.0 10.8 %copy.164 = bf16[2560,1536]{1,0:T(8,128)(2,1)} copy(bf16[2560,1536]{0,1:T(8,128)(2,1)} %bitcast.188) | data formatting | bytes 15728640 | tf_op jit(solution)/shard_map/dot_general | solution.py:1353
  232.8 5.6 fusion.50
  240.3 3.7 copy.233
  243.9 2.7 copy.232
  247.9 4.7 subtract_convert_fusion
  254.1 4.2 collective-permute-start.1
  258.3 2.3 collective-permute-start
  263.9 4.8 slice.213
  274.0 2.3 pad_maximum_fusion.2
  276.5 1.8 maximum_maximum_fusion
  278.4 3.0 fusion.6
  281.4 12.1 %fusion.90 = (f32[8,3,256]{2,1,0:T(4,128)S(1)}, f32[8,3,256,768]{2,3,1,0:T(8,128)}) fusion(pred[256,768]{0,1:T(8,128)(4,1)S(1)} %compare_and_fusion, bf16[256,8,3,64]{3,0,2,1:T(8,128)(2,1)} %copy-done.33, bf16[768,8,128]{2,0,1:T(8,128)(2,1)S(1)} %maximum_maximum_fusion), kind=kOutput, calls=%fused_computation.199 | convolution fusion | flops 627573504 | bytes 21651456 | tf_op jit(solution)/shard_map/sub | solution.py:1383
  294.1 8.6 fusion.39
  302.7 4.2 multiply_reduce_fusion
  308.2 112.6 %shard_map.392 = bf16[4,2,2,2,256,1536]{5,4,3,2,1,0:T(8,128)(2,1)} custom-call(bf16[256,1536]{1,0:T(8,128)(2,1)} %multiply_convert_fusion.1.refs_0_), custom_call_target="tpu_custom_call" | custom-call | bytes 50331648 | tf_op jit(solution)/shard_map/pallas_call | solution.py:405
  420.8 100.7 %shard_map.393 = (bf16[8192,1536]{1,0:T(8,128)(2,1)}, bf16[8192,1536]{1,0:T(8,128)(2,1)}, bf16[16,96,640]{2,1,0:T(8,128)(2,1)}, bf16[16,2,96,640]{3,2,1,0:T(8,128)(2,1)}) custom-call(f32[32,8,256]{2,1,0:T(8,128)} %stack.79.table_ref, bf16[8192,1536]{1,0:T(8,128)(2,1)} %bitcast.186, bf16[8192,1536]{1,0:T(8,128)(2,1)} %bitcast.213, bf16[3,1536,640]{2,1,0:T(8,128)(2,1)} %bitcast.214), custom_call_target="tpu_custom_call" | custom-call | flops 61404610560 | bytes 112459776 | tf_op jit(solution)/shard_map/pallas_call | solution.py:1256
  521.5 156.5 %shard_map.394 = (bf16[256,1536]{1,0:T(8,128)(2,1)}, bf16[2,4,2,256,768]{4,3,2,1,0:T(8,128)(2,1)}, bf16[2,4,2,256,768]{4,3,2,1,0:T(8,128)(2,1)}, bf16[16,2,96,640]{3,2,1,0:T(8,128)(2,1)}) custom-call(bf16[4,2,2,2,256,1536]{5,4,3,2,1,0:T(8,128)(2,1)} %bitcast.185, bf16[4,2,2,2,256,1536]{5,4,3,2,1,0:T(8,128)(2,1)} %bitcast.184, ...), custom_call_target="tpu_custom_call" | custom-call | flops 25165824 | bytes 50331648 | tf_op jit(solution)/shard_map/pallas_call | solution.py:804
  680.3 4.4 all-to-all-start
  687.6 3.8 convolution_convert_fusion.2
  692.5 12.1 %fusion.2 = (f32[8,3,256]{2,1,0:T(4,128)S(1)}, f32[8,768,256,3]{2,1,3,0:T(8,128)}) fusion(f32[8,3,256,768]{2,3,1,0:T(8,128)} %get-tuple-element.190, f32[8,3,256]{2,1,0:T(4,128)S(1)} %get-tuple-element.189, bf16[256,8,3,64]{0,3,2,1:T(8,128)(2,1)S(1)} %bitcast.204, bf16[768,8,128]{2,0,1:T(8,128)(2,1)S(1)} %copy-done.24), kind=kOutput, calls=%fused_computation.5 | convolution fusion | flops 618129408 | bytes 40157184 | tf_op jit(solution)/shard_map/qjid,kjd->jiqk/dot_general | solution.py:1416
  704.6 13.1 %fusion.4 = bf16[8,3,256,768]{2,3,1,0:T(8,128)(2,1)S(1)} fusion(f32[8,768,256,3]{2,1,3,0:T(8,128)} %get-tuple-element.194, f32[8,3,256]{2,1,0:T(4,128)S(1)} %get-tuple-element.193, f32[8,3,256,768]{2,3,1,0:T(8,128)} %get-tuple-element.190, f32[8,3,256]{2,1,0:T(4,128)S(1)} %get-tuple-element.189), kind=kLoop, calls=%fused_computation.7 | loop fusion | flops 18874368 | bytes 47235072 | tf_op jit(solution)/shard_map/convert_element_type | solution.py:1420
  717.7 2.6 fusion.15
  720.3 12.0 %fusion.18 = f32[768,8,64]{2,0,1:T(8,128)} fusion(bf16[256,8,3,64]{0,3,2,1:T(8,128)(2,1)} %bitcast.205, f32[8,3,256,768]{2,3,1,0:T(8,128)} %get-tuple-element.190, f32[8,3,256]{2,1,0:T(4,128)S(1)} %get-tuple-element.189), kind=kOutput, calls=%fused_computation.52 | convolution fusion | flops 613416960 | bytes 21258240 | tf_op jit(solution)/shard_map/jiqk,qjid->kjd/dot_general | solution.py:1429
  732.3 2.7 maximum_convert_fusion
  738.8 3.0 multiply_bitcast_fusion
  741.9 4.9 convolution_convert_fusion.1
  746.8 27.5 %collective-permute-done.3 = bf16[256,8,128]{2,0,1:T(8,128)(2,1)} collective-permute-done((bf16[256,8,128]{2,0,1:T(8,128)(2,1)}, bf16[256,8,128]{2,0,1:T(8,128)(2,1)}, u32[]{:S(2)}, u32[]{:S(2)}) %collective-permute-start.3) | collective-permute-done | bytes 524320 | tf_op jit(solution)/shard_map/ppermute | solution.py:89
  780.4 3.2 multiply_subtract_fusion
  785.7 3.2 copy-done.7
  789.0 3.6 shard_map.395
  792.6 2.2 slice_bitcast_fusion
  794.8 1.8 collective-permute-start.5
  796.5 7.3 fusion.38
  806.8 4.0 convolution_convert_fusion
  810.8 8.0 fusion.5
  818.8 27.1 %shard_map.398 = (f32[20,96,512]{2,1,0:T(8,128)}, f32[20,96,512]{2,1,0:T(8,128)}, f32[20,96,512]{2,1,0:T(8,128)}, f32[20,96,512]{2,1,0:T(8,128)}, f32[20,96,512]...) custom-call(f32[20,96,512]{2,1,0:T(8,128)} %refs_0_.1, ...), custom_call_target="tpu_custom_call" | custom-call | flops 58982400 | bytes 78643200 | tf_op jit(solution)/shard_map/pallas_call | solution.py:1087
  847.0 2.9 shard_map.396.refs_0_
  851.6 96.1 %shard_map.397 = (bf16[48,4352]{1,0:T(8,128)(2,1)}, f32[256,1536]{1,0:T(8,128)}) custom-call(bf16[4,2,2,2,48,4352]{5,4,3,2,1,0:T(8,128)(2,1)} %bitcast.183, bf16[4,2,256,768]{3,2,1,0:T(8,128)(2,1)} %copy-done.6), custom_call_target="tpu_custom_call" | custom-call | flops 13369344 | bytes 26738688 | tf_op jit(solution)/shard_map/pallas_call | solution.py:804
  953.5 5.2 concatenate.47
  959.3 18.0 %shard_map.399 = f32[4,2,2,2,8,128]{5,4,3,2,1,0:T(8,128)} custom-call(f32[8,128]{1,0:T(8,128)} %pad.16.src_ref), custom_call_target="tpu_custom_call" | custom-call | tf_op jit(solution)/shard_map/pallas_call | solution.py:889
  985.0 6.5 multiply_subtract_fusion.2
  993.0 2.1 fusion.29
  997.1 8.5 subtract_bitcast_fusion
  (234 shorter events, 60.6 us)
Async XLA Ops:
  2.7 230.0 %copy-start.54 = (f32[256]{0:T(256)}, f32[256]{0:T(256)S(1)}, u32[]{:S(2)}) copy-start(f32[256]{0:T(256)S(1)} %add_rsqrt_fusion.1) | copy-start | bytes 3076
  222.0 10.8 %copy-start.51 = (f32[1536]{0:T(1024)}, f32[1536]{0:T(1024)S(1)}, u32[]{:S(2)}) copy-start(f32[1536]{0:T(1024)S(1)} %reshape.290) | copy-start | bytes 18436
  222.0 10.8 %copy-start.18 = (bf16[256,1536]{1,0:T(8,128)(2,1)S(1)}, bf16[256,1536]{1,0:T(8,128)(2,1)}, u32[]{:S(2)}) copy-start(bf16[256,1536]{1,0:T(8,128)(2,1)} %param.23) | copy-start | bytes 2359300
  247.9 4.7 copy-start.37
  252.6 8.0 copy-start.58
  252.7 10.9 %copy-start.61 = (f32[2,48]{1,0:T(2,128)S(1)}, f32[2,48]{1,0:T(2,128)}, u32[]{:S(2)}) copy-start(f32[2,48]{1,0:T(2,128)} %param.35) | copy-start | bytes 1156
  252.7 10.9 %copy-start.62 = (f32[2,48]{1,0:T(2,128)S(1)}, f32[2,48]{1,0:T(2,128)}, u32[]{:S(2)}) copy-start(f32[2,48]{1,0:T(2,128)} %param.36) | copy-start | bytes 1156
  254.1 22.4 %collective-permute-start.1 = (bf16[256,8,128]{2,0,1:T(8,128)(2,1)}, bf16[256,8,128]{2,0,1:T(8,128)(2,1)}, u32[]{:S(2)}, u32[]{:S(2)}) collective-permute-start(bf16[256,8,128]{2,0,1:T(8,128)(2,1)} %pad_maximum_fusion.3), channel_id=1, source_target_pairs={{0,1},{1,2},{2,3},{3,4},{4,5},{5,6},{6,7},{7,8},{8,9},{9,10},{10,1... | collective-permute-start | bytes 1572872 | tf_op jit(solution)/shard_map/ppermute | solution.py:89
  258.3 18.2 %collective-permute-start = (bf16[256,8,128]{2,0,1:T(8,128)(2,1)}, bf16[256,8,128]{2,0,1:T(8,128)(2,1)}, u32[]{:S(2)}, u32[]{:S(2)}) collective-permute-start(bf16[256,8,128]{2,0,1:T(8,128)(2,1)} %pad_maximum_fusion.3), channel_id=1, source_target_pairs={{0,2},{1,3},{2,4},{3,5},{4,6},{5,7},{6,8},{7,9},{8,10},{9,11},{10,... | collective-permute-start | bytes 1572872 | tf_op jit(solution)/shard_map/ppermute | solution.py:89
  278.4 15.7 %copy-start.23 = (bf16[768,8,128]{2,0,1:T(8,128)(2,1)}, bf16[768,8,128]{2,0,1:T(8,128)(2,1)S(1)}, u32[]{:S(2)}) copy-start(bf16[768,8,128]{2,0,1:T(8,128)(2,1)S(1)} %maximum_maximum_fusion) | copy-start | bytes 4718596
  294.1 8.6 copy-start.19
  302.7 4.2 copy-start.40
  306.9 377.8 %copy-start.9 = (f32[256,1536]{1,0:T(8,128)}, f32[256,1536]{1,0:T(8,128)S(1)}, u32[]{:S(2)}) copy-start(f32[256,1536]{1,0:T(8,128)S(1)} %get-tuple-element.192) | copy-start | bytes 4718596
  678.0 6.7 copy-start.29
  680.3 138.5 %all-to-all-start = ((bf16[16,96,640]{2,1,0:T(8,128)(2,1)}), bf16[16,96,640]{2,1,0:T(8,128)(2,1)}, u32[]{:S(2)}, u32[]{:S(2)}) async-start(bf16[16,96,640]{2,1,0:T(8,128)(2,1)} %get-tuple-element.57), calls=%async_computation | async-start | bytes 3932160 | tf_op jit(solution)/shard_map/all_to_all | solution.py:1128
  687.6 4.9 copy-start.24
  691.7 12.9 %copy-start.39 = (bf16[256,1536]{0,1:T(8,128)(2,1)}, bf16[256,1536]{0,1:T(8,128)(2,1)S(1)}, u32[]{:S(2)}) copy-start(bf16[256,1536]{0,1:T(8,128)(2,1)S(1)} %copy.173) | copy-start | bytes 2359300
  691.7 94.0 %collective-permute-start.4 = (bf16[2,4,2,256,768]{4,3,2,1,0:T(8,128)(2,1)}, bf16[2,4,2,256,768]{4,3,2,1,0:T(8,128)(2,1)}, u32[]{:S(2)}, u32[]{:S(2)}) collective-permute-start(bf16[2,4,2,256,768]{4,3,2,1,0:T(8,128)(2,1)} %get-tuple-element.55), channel_id=1, source_target_pairs={{0,1},{1,0},{2,6},{3,7},{4,5},{5,4},{6,2},{7,3},{8,9},{9,8},{10,14... | collective-permute-start | bytes 18874376 | tf_op jit(solution)/shard_map/ppermute | solution.py:428
  704.6 13.1 %copy-start.34 = (bf16[256,8,3,64]{3,0,2,1:T(8,128)(2,1)S(1)}, bf16[256,8,3,64]{3,0,2,1:T(8,128)(2,1)}, u32[]{:S(2)}) copy-start(bf16[256,8,3,64]{3,0,2,1:T(8,128)(2,1)} %copy-done.33) | copy-start | bytes 2359300
  720.3 12.0 %copy-start.15 = (f32[768,8,64]{2,0,1:T(8,128)}, f32[768,8,64]{2,0,1:T(8,128)S(1)}, u32[]{:S(2)}) copy-start(f32[768,8,64]{2,0,1:T(8,128)S(1)} %fusion.15) | copy-start | bytes 4718596
  732.3 6.5 copy-start.25
  736.1 10.7 %collective-permute-start.2 = (bf16[256,8,128]{2,0,1:T(8,128)(2,1)}, bf16[256,8,128]{2,0,1:T(8,128)(2,1)}, u32[]{:S(2)}, u32[]{:S(2)}) collective-permute-start(bf16[256,8,128]{2,0,1:T(8,128)(2,1)} %get-tuple-element.152), channel_id=1, source_target_pairs={{2,0},{3,1},{4,2},{5,3},{6,4},{7,5},{8,6},{9,7},{10,8},{11,9},{12,... | collective-permute-start | bytes 1572872 | tf_op jit(solution)/shard_map/ppermute | solution.py:89
  737.4 4.5 copy-start.12
  737.4 36.9 %collective-permute-start.3 = (bf16[256,8,128]{2,0,1:T(8,128)(2,1)}, bf16[256,8,128]{2,0,1:T(8,128)(2,1)}, u32[]{:S(2)}, u32[]{:S(2)}) collective-permute-start(bf16[256,8,128]{2,0,1:T(8,128)(2,1)} %get-tuple-element.153), channel_id=1, source_target_pairs={{1,0},{2,1},{3,2},{4,3},{5,4},{6,5},{7,6},{8,7},{9,8},{10,9},{11,1... | collective-permute-start | bytes 1572872 | tf_op jit(solution)/shard_map/ppermute | solution.py:89
  741.8 43.9 %copy-start.8 = (f32[8,64]{1,0:T(8,128)}, f32[8,64]{1,0:T(8,128)S(1)}, u32[]{:S(2)}) copy-start(f32[8,64]{1,0:T(8,128)S(1)} %slice_bitcast_fusion.14.anchor_ref.refs_11_) | copy-start | bytes 6148
  741.9 32.4 %copy-start.16 = (f32[768,8,64]{2,0,1:T(8,128)S(1)}, f32[768,8,64]{2,0,1:T(8,128)}, u32[]{:S(2)}) copy-start(f32[768,8,64]{2,0,1:T(8,128)} %copy-done.15) | copy-start | bytes 4718596
  741.9 32.4 %copy-start.17 = (f32[768,8,64]{2,0,1:T(8,128)S(1)}, f32[768,8,64]{2,0,1:T(8,128)}, u32[]{:S(2)}) copy-start(f32[768,8,64]{2,0,1:T(8,128)} %fusion.18) | copy-start | bytes 4718596
  785.7 18.2 %copy-start.26 = (bf16[256,8,320]{0,2,1:T(8,128)(2,1)}, bf16[256,8,320]{0,2,1:T(8,128)(2,1)S(1)}, u32[]{:S(2)}) copy-start(bf16[256,8,320]{0,2,1:T(8,128)(2,1)S(1)} %maximum_convert_fusion.1) | copy-start | bytes 3932164
  794.8 52.3 %collective-permute-start.5 = (bf16[4,2,256,768]{3,2,1,0:T(8,128)(2,1)}, bf16[4,2,256,768]{3,2,1,0:T(8,128)(2,1)}, u32[]{:S(2)}, u32[]{:S(2)}) collective-permute-start(bf16[4,2,256,768]{3,2,1,0:T(8,128)(2,1)} %get-tuple-element.146), channel_id=1, source_target_pairs={{0,4},{1,5},{2,3},{3,2},{4,0},{5,1},{6,7},{7,6},{8,12},{9,13},{10,... | collective-permute-start | bytes 9437192 | tf_op jit(solution)/shard_map/ppermute | solution.py:428
  796.5 7.4 copy-start.53
  851.6 97.4 %copy-start.30 = (f32[1536,48]{0,1:T(8,128)S(1)}, f32[1536,48]{0,1:T(8,128)}, u32[]{:S(2)}) copy-start(f32[1536,48]{0,1:T(8,128)} %param.31) | copy-start | bytes 884740
  851.6 97.4 %copy-start.43 = (f32[1536,48]{0,1:T(8,128)S(1)}, f32[1536,48]{0,1:T(8,128)}, u32[]{:S(2)}) copy-start(f32[1536,48]{0,1:T(8,128)} %param.33) | copy-start | bytes 884740
  851.6 97.4 %copy-start.44 = (f32[1536,48]{0,1:T(8,128)S(1)}, f32[1536,48]{0,1:T(8,128)}, u32[]{:S(2)}) copy-start(f32[1536,48]{0,1:T(8,128)} %param.32) | copy-start | bytes 884740
  947.8 4.2 copy-start.45
  947.8 4.1 copy-start.46
  947.8 4.1 copy-start.47
  947.9 5.7 copy-start.60
  952.0 53.7 %copy-start.31 = (f32[48,2560]{1,0:T(8,128)}, f32[48,2560]{1,0:T(8,128)S(1)}, u32[]{:S(2)}) copy-start(f32[48,2560]{1,0:T(8,128)S(1)} %get-tuple-element.140) | copy-start | bytes 1474564
  952.0 53.6 %copy-start.32 = (f32[48,2560]{1,0:T(8,128)}, f32[48,2560]{1,0:T(8,128)S(1)}, u32[]{:S(2)}) copy-start(f32[48,2560]{1,0:T(8,128)S(1)} %get-tuple-element.141) | copy-start | bytes 1474564
  978.9 12.7 %copy-start.63 = (f32[24]{0:T(128)}, f32[24]{0:T(128)S(1)}, u32[]{:S(2)}) copy-start(f32[24]{0:T(128)S(1)} %maximum_divide_fusion) | copy-start | bytes 292
  985.0 7.3 copy-start.59
  985.0 7.9 copy-start.10
  985.0 7.9 copy-start.13
  985.0 7.9 copy-start.21
  985.0 7.9 copy-start.35
  985.0 7.9 copy-start.36
  985.0 7.9 copy-start.57
  992.9 4.2 copy-start.4
  (24 other events, 69.1 us)
